TPU v7x, 32 devices: a whole 2x2x4 slice. The times are simulated.
32 devices in a mesh: dp: 8 (over y, x, core), ctx: 4 (over z).
Axes of the slice: x: 2, y: 2, z: 4, core: 2. Of those that a mesh axis runs over, the one named last changes fastest.
Arguments:
- keys_a: bfloat16 [8, 512, 2560], P('dp', 'ctx'), may hold values from -6 to 6
- values_a: bfloat16 [8, 512, 2560], P('dp', 'ctx'), may hold values from -6 to 6
- queries_b: bfloat16 [8, 512, 2560], P('dp', 'ctx'), may hold values from -6 to 6
- grad_out: bfloat16 [8, 512, 2560], P('dp', 'ctx'), may hold values from -1.5 to 1.5
- state_start: float32 [3, 20, 128, 128], P(None, None, 'ctx'), may hold values from -0.5 to 0.5
- state_next: float32 [8, 3, 20, 128, 128], P('dp', None, None, 'ctx'), may hold values from -0.5 to 0.5
Outputs:
- grad_keys: bfloat16 [8, 512, 2560], P('dp', 'ctx')
- grad_values: bfloat16 [8, 512, 2560], P('dp', 'ctx')
- grad_state: float32 [3, 20, 128, 128], P(None, None, 'ctx')
All inputs are finite; a program needn't handle non-finite values.
Results may differ from a plain program's by a relative error of at most 0.033.
Values may be sent and summed in bfloat16 or wider, within the bound.
No kernel may reach another device: no remote copies, remote signals or barrier semaphores. Data moves between devices by JAX's collectives and lax.ppermute only.
A program may use at most 128 MiB of HBM per device.

v0:
```python
import jax
import jax.numpy as jnp
from jax import lax
from jax.sharding import PartitionSpec as P

D = 128
H = 20
F = 128
NS_STEPS = 2


step_rate = 4.0
coef_a = 3.4445
coef_b = -4.775
coef_c = 2.0315


def field_grad(weights, inputs, targets):
    gate_pre = jnp.einsum("thd,hdf->thf", inputs, weights[0], preferred_element_type=jnp.float32)
    up_pre = jnp.einsum("thd,hdf->thf", inputs, weights[1], preferred_element_type=jnp.float32)
    target_proj = jnp.einsum(
        "thd,hdf->thf", targets, weights[2], preferred_element_type=jnp.float32
    )
    sigmoid_val = jax.nn.sigmoid(gate_pre)
    swish_val = gate_pre * sigmoid_val
    hidden = (swish_val * up_pre).astype(jnp.bfloat16)
    d_gate = (target_proj * up_pre * sigmoid_val * (1.0 + gate_pre * (1.0 - sigmoid_val))).astype(
        jnp.bfloat16
    )
    d_up = (target_proj * swish_val).astype(jnp.bfloat16)
    grad_a = jnp.einsum("thd,thf->hdf", inputs, d_gate, preferred_element_type=jnp.float32)
    grad_b = jnp.einsum("thd,thf->hdf", inputs, d_up, preferred_element_type=jnp.float32)
    grad_c = jnp.einsum("thd,thf->hdf", targets, hidden, preferred_element_type=jnp.float32)
    return jnp.stack([grad_a, grad_b, grad_c])


def newton(gradients):
    scale_norm = jnp.sqrt(jnp.sum(gradients * gradients, axis=(1, 2), keepdims=True) + 1e-06)
    iterate = (gradients / scale_norm).astype(jnp.bfloat16)
    for repeat in range(NS_STEPS):
        gram_block = jnp.einsum(
            "mdf,mef->mde", iterate, iterate, preferred_element_type=jnp.float32
        ).astype(jnp.bfloat16)
        square = jnp.einsum(
            "mde,mek->mdk", gram_block, gram_block, preferred_element_type=jnp.float32
        )
        poly_term = (coef_b * gram_block.astype(jnp.float32) + coef_c * square).astype(jnp.bfloat16)
        mixed = jnp.einsum("mde,mef->mdf", poly_term, iterate, preferred_element_type=jnp.float32)
        iterate = (coef_a * iterate.astype(jnp.float32) + mixed).astype(jnp.bfloat16)
    return iterate


def local(keys_a, values_a, queries_b, grad_out, state_start, state_next):
    tokens = keys_a.shape[1]
    block_shape = (tokens, H, D)
    key_rows = keys_a.reshape(block_shape)
    value_rows = values_a.reshape(block_shape)
    query_rows = queries_b.reshape(block_shape)
    out_rows = grad_out.reshape(block_shape)
    clip_next = state_next[0]
    ctx_count = lax.axis_size("ctx")
    per_dev = (H + ctx_count - 1) // ctx_count
    head_pad = per_dev * ctx_count - H
    token_pad = ((0, 0), (0, head_pad), (0, 0))
    state_pad = ((0, 0), (0, head_pad), (0, 0), (0, 0))
    padded = [jnp.pad(rows, token_pad) for rows in (key_rows, value_rows, query_rows, out_rows)]
    key_all, value_all, query_all, out_all = (
        lax.all_to_all(padded[0], "ctx", split_axis=1, concat_axis=0, tiled=True),
        lax.all_to_all(padded[1], "ctx", split_axis=1, concat_axis=0, tiled=True),
        lax.all_to_all(padded[2], "ctx", split_axis=1, concat_axis=0, tiled=True),
        lax.all_to_all(padded[3], "ctx", split_axis=1, concat_axis=0, tiled=True),
    )
    start_pad = jnp.pad(state_start.astype(jnp.bfloat16), state_pad)
    next_pad = jnp.pad(clip_next.astype(jnp.bfloat16), state_pad)
    start_own, next_own = (
        lax.all_to_all(start_pad, "ctx", split_axis=1, concat_axis=2, tiled=True),
        lax.all_to_all(next_pad, "ctx", split_axis=1, concat_axis=2, tiled=True),
    )
    blocks = (ctx_count, tokens, per_dev, D)
    key_blocks = key_all.reshape(blocks)
    value_blocks = value_all.reshape(blocks)
    query_blocks = query_all.reshape(blocks)
    out_blocks = out_all.reshape(blocks)
    parts_g = jax.vmap(field_grad, in_axes=(None, 0, 0))(start_own, key_blocks, value_blocks)
    total_g = jnp.sum(parts_g.astype(jnp.bfloat16).astype(jnp.float32), axis=0)
    parts_s = jax.vmap(field_grad, in_axes=(None, 0, 0))(next_own, query_blocks, out_blocks)
    total_s = jnp.sum(parts_s.astype(jnp.bfloat16).astype(jnp.float32), axis=0)
    own_slots = (3 * per_dev, D, F)
    d_update = (step_rate * total_s).astype(jnp.bfloat16).reshape(own_slots)
    unused, pullback = jax.vjp(newton, total_g.reshape(own_slots))
    d_field = pullback(d_update)[0].reshape(total_g.shape)

    def backward(key_block, value_block):
        unused_out, pull_block = jax.vjp(field_grad, start_own, key_block, value_block)
        return pull_block(d_field)

    d_start, d_keys, d_values = jax.vmap(backward)(key_blocks, value_blocks)
    summed = (parts_s + d_start.astype(jnp.float32)).astype(jnp.bfloat16).astype(jnp.float32)
    clip_heads = jnp.sum(summed, axis=0)
    back_shape = (ctx_count * tokens, per_dev, D)
    keys_back, values_back = (
        lax.all_to_all(d_keys.reshape(back_shape), "ctx", split_axis=0, concat_axis=1, tiled=True),
        lax.all_to_all(
            d_values.reshape(back_shape), "ctx", split_axis=0, concat_axis=1, tiled=True
        ),
    )
    rows_back = lax.all_to_all(
        clip_heads.astype(jnp.bfloat16), "ctx", split_axis=2, concat_axis=1, tiled=True
    ).astype(clip_heads.dtype)
    state_shard = rows_back[:, :H]
    d_keys_out = keys_back[:, :H].reshape(keys_a.shape)
    d_values_out = values_back[:, :H].reshape(values_a.shape)
    state_total = lax.psum(state_shard.astype(jnp.bfloat16), "dp").astype(jnp.float32)
    grad_state = state_total / lax.axis_size("dp")
    return (d_keys_out, d_values_out, grad_state)


def solution(mesh):
    placed = (
        P("dp", "ctx", None),
        P("dp", "ctx", None),
        P("dp", "ctx", None),
        P("dp", "ctx", None),
        P(None, None, "ctx", None),
        P("dp", None, None, "ctx", None),
    )
    return jax.shard_map(
        local,
        mesh=mesh,
        in_specs=placed,
        out_specs=(P("dp", "ctx", None), P("dp", "ctx", None), P(None, None, "ctx", None)),
        check_vma=False,
    )
```

profile of v0, /device:TPU:0, one launch (start us, length us, event | category | flops | bytes accessed | tf_op | source)
XLA Modules:
  0.0 285.1 jit_solution(10650306908713625781)
XLA Ops:
  7.2 2.1 copy.398
  9.3 6.3 %all-to-all-start.3 = ((bf16[3,20,32,128]{3,2,0,1:T(8,128)(2,1)}), bf16[3,20,32,128]{3,2,0,1:T(8,128)(2,1)S(1)}, u32[]{:S(2)}, u32[]{:S(2)}) async-start(bf16[3,20,32,128]{3,2,0,1:T(8,128)(2,1)} %copy.398), calls=%async_computation.3 | async-start | bytes 983040 | tf_op jit(solution)/shard_map/all_to_all | solution.py:76
  16.5 12.9 %all-to-all-done.3 = bf16[3,20,32,128]{3,2,0,1:T(8,128)(2,1)S(1)} async-done(((bf16[3,20,32,128]{3,2,0,1:T(8,128)(2,1)}), bf16[3,20,32,128]{3,2,0,1:T(8,128)(2,1)S(1)}, u32[]{:S(2)}, u32[]{:S(2)}) %all-to-all-start.3) | async-done | bytes 491552 | tf_op jit(solution)/shard_map/all_to_all | solution.py:76
  29.4 3.5 %all-to-all-start = ((bf16[3,20,32,128]{3,2,0,1:T(8,128)(2,1)}), bf16[3,20,32,128]{3,2,0,1:T(8,128)(2,1)S(1)}, u32[]{:S(2)}, u32[]{:S(2)}) async-start(bf16[3,20,32,128]{3,2,0,1:T(8,128)(2,1)} %bitcast.382), calls=%async_computation | async-start | bytes 983040 | tf_op jit(solution)/shard_map/all_to_all | solution.py:77
  32.9 1.1 copy.267
  34.0 12.2 %all-to-all-done = bf16[3,20,32,128]{3,2,0,1:T(8,128)(2,1)S(1)} async-done(((bf16[3,20,32,128]{3,2,0,1:T(8,128)(2,1)}), bf16[3,20,32,128]{3,2,0,1:T(8,128)(2,1)S(1)}, u32[]{:S(2)}, u32[]{:S(2)}) %all-to-all-start) | async-done | bytes 491552 | tf_op jit(solution)/shard_map/all_to_all | solution.py:77
  46.2 3.5 %all-to-all-start.5 = ((bf16[128,20,128]{0,2,1:T(8,128)(2,1)}), bf16[128,20,128]{0,2,1:T(8,128)(2,1)S(1)}, u32[]{:S(2)}, u32[]{:S(2)}) async-start(bf16[128,20,128]{0,2,1:T(8,128)(2,1)} %bitcast.41), calls=%async_computation.5 | async-start | bytes 1310720 | tf_op jit(solution)/shard_map/all_to_all | solution.py:68
  49.7 1.1 copy.262
  50.8 15.7 %all-to-all-done.5 = bf16[128,20,128]{0,2,1:T(8,128)(2,1)S(1)} async-done(((bf16[128,20,128]{0,2,1:T(8,128)(2,1)}), bf16[128,20,128]{0,2,1:T(8,128)(2,1)S(1)}, u32[]{:S(2)}, u32[]{:S(2)}) %all-to-all-start.5) | async-done | bytes 655392 | tf_op jit(solution)/shard_map/all_to_all | solution.py:68
  66.4 3.5 %all-to-all-start.4 = ((bf16[128,20,128]{0,2,1:T(8,128)(2,1)}), bf16[128,20,128]{0,2,1:T(8,128)(2,1)S(1)}, u32[]{:S(2)}, u32[]{:S(2)}) async-start(bf16[128,20,128]{0,2,1:T(8,128)(2,1)} %bitcast.34), calls=%async_computation.4 | async-start | bytes 1310720 | tf_op jit(solution)/shard_map/all_to_all | solution.py:69
  69.9 1.1 copy.246
  71.0 2.2 copy.241
  75.8 10.8 %all-to-all-done.4 = bf16[128,20,128]{0,2,1:T(8,128)(2,1)S(1)} async-done(((bf16[128,20,128]{0,2,1:T(8,128)(2,1)}), bf16[128,20,128]{0,2,1:T(8,128)(2,1)S(1)}, u32[]{:S(2)}, u32[]{:S(2)}) %all-to-all-start.4) | async-done | bytes 655392 | tf_op jit(solution)/shard_map/all_to_all | solution.py:69
  86.7 3.5 %all-to-all-start.2 = ((bf16[128,20,128]{0,2,1:T(8,128)(2,1)}), bf16[128,20,128]{0,2,1:T(8,128)(2,1)S(1)}, u32[]{:S(2)}, u32[]{:S(2)}) async-start(bf16[128,20,128]{0,2,1:T(8,128)(2,1)} %bitcast.399), calls=%async_computation.2 | async-start | bytes 1310720 | tf_op jit(solution)/shard_map/all_to_all | solution.py:70
  90.1 1.1 copy.264
  92.7 2.1 fusion.29
  97.7 9.2 %all-to-all-done.2 = bf16[128,20,128]{0,2,1:T(8,128)(2,1)S(1)} async-done(((bf16[128,20,128]{0,2,1:T(8,128)(2,1)}), bf16[128,20,128]{0,2,1:T(8,128)(2,1)S(1)}, u32[]{:S(2)}, u32[]{:S(2)}) %all-to-all-start.2) | async-done | bytes 655392 | tf_op jit(solution)/shard_map/all_to_all | solution.py:70
  106.9 4.3 %all-to-all-start.1 = ((bf16[128,20,128]{0,2,1:T(8,128)(2,1)}), bf16[128,20,128]{0,2,1:T(8,128)(2,1)}, u32[]{:S(2)}, u32[]{:S(2)}) async-start(bf16[128,20,128]{0,2,1:T(8,128)(2,1)} %bitcast.398), calls=%async_computation.1 | async-start | bytes 1310720 | tf_op jit(solution)/shard_map/all_to_all | solution.py:71
  111.3 1.1 copy.248
  115.2 12.7 %all-to-all-done.1 = bf16[128,20,128]{0,2,1:T(8,128)(2,1)} async-done(((bf16[128,20,128]{0,2,1:T(8,128)(2,1)}), bf16[128,20,128]{0,2,1:T(8,128)(2,1)}, u32[]{:S(2)}, u32[]{:S(2)}) %all-to-all-start.1) | async-done | bytes 655392 | tf_op jit(solution)/shard_map/all_to_all | solution.py:71
  127.9 2.2 copy.243
  130.1 1.5 convolution_bitcast_fusion.4
  135.0 2.1 convolution_bitcast_fusion
  140.5 1.1 convolution_convert_fusion.17
  141.7 1.1 convolution_convert_fusion.16
  143.7 2.5 fusion.66
  148.3 1.1 convolution_convert_fusion.13
  150.6 2.2 fusion.71
  156.6 2.1 fusion.16
  162.5 1.4 copy.307
  163.9 3.6 %all-to-all-start.8 = ((bf16[3,5,128,128]{3,0,1,2:T(4,128)(2,1)}), bf16[3,5,128,128]{3,0,1,2:T(4,128)(2,1)S(1)}, u32[]{:S(2)}, u32[]{:S(2)}) async-start(bf16[3,5,128,128]{3,0,1,2:T(4,128)(2,1)} %copy.307), calls=%async_computation.8 | async-start | bytes 1310720 | tf_op jit(solution)/shard_map/all_to_all | solution.py:107
  167.5 1.1 copy.296
  168.7 1.1 copy.286
  169.7 1.5 fusion.115
  171.7 1.4 copy.298
  173.1 11.2 %all-to-all-done.8 = bf16[3,5,128,128]{3,0,1,2:T(4,128)(2,1)S(1)} async-done(((bf16[3,5,128,128]{3,0,1,2:T(4,128)(2,1)}), bf16[3,5,128,128]{3,0,1,2:T(4,128)(2,1)S(1)}, u32[]{:S(2)}, u32[]{:S(2)}) %all-to-all-start.8) | async-done | bytes 491552 | tf_op jit(solution)/shard_map/all_to_all | solution.py:107
  184.3 3.5 %all-to-all-start.7 = ((bf16[512,5,128]{2,1,0:T(8,128)(2,1)}), bf16[512,5,128]{2,1,0:T(8,128)(2,1)S(1)}, u32[]{:S(2)}, u32[]{:S(2)}) async-start(bf16[512,5,128]{2,1,0:T(8,128)(2,1)} %copy.298), calls=%async_computation.7 | async-start | bytes 2097152 | tf_op jit(solution)/shard_map/all_to_all | solution.py:103
  187.8 2.7 fusion.113
  190.5 1.1 copy.287
  191.6 1.6 fusion.114
  194.8 1.5 copy.293
  196.3 16.7 %all-to-all-done.7 = bf16[512,5,128]{2,1,0:T(8,128)(2,1)S(1)} async-done(((bf16[512,5,128]{2,1,0:T(8,128)(2,1)}), bf16[512,5,128]{2,1,0:T(8,128)(2,1)S(1)}, u32[]{:S(2)}, u32[]{:S(2)}) %all-to-all-start.7) | async-done | bytes 655392 | tf_op jit(solution)/shard_map/all_to_all | solution.py:103
  213.0 3.5 %all-to-all-start.6 = ((bf16[512,5,128]{2,1,0:T(8,128)(2,1)}), bf16[512,5,128]{2,1,0:T(8,128)(2,1)S(1)}, u32[]{:S(2)}, u32[]{:S(2)}) async-start(bf16[512,5,128]{2,1,0:T(8,128)(2,1)} %copy.293), calls=%async_computation.6 | async-start | bytes 2097152 | tf_op jit(solution)/shard_map/all_to_all | solution.py:102
  218.2 1.1 copy.311
  219.2 22.5 %all-to-all-done.6 = bf16[512,5,128]{2,1,0:T(8,128)(2,1)S(1)} async-done(((bf16[512,5,128]{2,1,0:T(8,128)(2,1)}), bf16[512,5,128]{2,1,0:T(8,128)(2,1)S(1)}, u32[]{:S(2)}, u32[]{:S(2)}) %all-to-all-start.6) | async-done | bytes 655392 | tf_op jit(solution)/shard_map/all_to_all | solution.py:102
  242.3 1.1 copy.310
  243.4 32.8 %all-reduce.5.cloned.1.call-done = bf16[3,20,32,128]{3,2,1,0:T(8,128)(2,1)} async-done(((bf16[3,20,32,128]{3,2,1,0:T(8,128)(2,1)}), bf16[3,20,32,128]{3,2,1,0:T(8,128)(2,1)}) %all-reduce.5.cloned.1.call-update) | async-done | bytes 491536 | tf_op jit(solution)/shard_map/psum | solution.py:113
  276.2 2.1 convert_multiply_fusion.1
  (166 shorter events, 32.9 us)
Async XLA Ops:
  7.2 8.5 %copy-start.43 = (f32[1,3,20,32,128]{4,3,2,1,0:T(8,128)S(1)}, f32[1,3,20,32,128]{4,3,2,1,0:T(8,128)}, u32[]{:S(2)}) copy-start(f32[1,3,20,32,128]{4,3,2,1,0:T(8,128)} %param.11) | copy-start | bytes 2949124
  9.3 20.1 %all-to-all-start.3 = ((bf16[3,20,32,128]{3,2,0,1:T(8,128)(2,1)}), bf16[3,20,32,128]{3,2,0,1:T(8,128)(2,1)S(1)}, u32[]{:S(2)}, u32[]{:S(2)}) async-start(bf16[3,20,32,128]{3,2,0,1:T(8,128)(2,1)} %copy.398), calls=%async_computation.3 | async-start | bytes 983040 | tf_op jit(solution)/shard_map/all_to_all | solution.py:76
  15.6 17.3 %copy-start.48 = (bf16[1,128,2560]{2,1,0:T(8,128)(2,1)S(1)}, bf16[1,128,2560]{2,1,0:T(8,128)(2,1)}, u32[]{:S(2)}) copy-start(bf16[1,128,2560]{2,1,0:T(8,128)(2,1)} %param.6) | copy-start | bytes 1966084
  29.4 16.7 %all-to-all-start = ((bf16[3,20,32,128]{3,2,0,1:T(8,128)(2,1)}), bf16[3,20,32,128]{3,2,0,1:T(8,128)(2,1)S(1)}, u32[]{:S(2)}, u32[]{:S(2)}) async-start(bf16[3,20,32,128]{3,2,0,1:T(8,128)(2,1)} %bitcast.382), calls=%async_computation | async-start | bytes 983040 | tf_op jit(solution)/shard_map/all_to_all | solution.py:77
  32.9 16.7 %copy-start.49 = (bf16[1,128,2560]{2,1,0:T(8,128)(2,1)S(1)}, bf16[1,128,2560]{2,1,0:T(8,128)(2,1)}, u32[]{:S(2)}) copy-start(bf16[1,128,2560]{2,1,0:T(8,128)(2,1)} %param.7) | copy-start | bytes 1966084
  46.2 20.2 %all-to-all-start.5 = ((bf16[128,20,128]{0,2,1:T(8,128)(2,1)}), bf16[128,20,128]{0,2,1:T(8,128)(2,1)S(1)}, u32[]{:S(2)}, u32[]{:S(2)}) async-start(bf16[128,20,128]{0,2,1:T(8,128)(2,1)} %bitcast.41), calls=%async_computation.5 | async-start | bytes 1310720 | tf_op jit(solution)/shard_map/all_to_all | solution.py:68
  49.7 20.2 %copy-start.50 = (bf16[1,128,2560]{2,1,0:T(8,128)(2,1)S(1)}, bf16[1,128,2560]{2,1,0:T(8,128)(2,1)}, u32[]{:S(2)}) copy-start(bf16[1,128,2560]{2,1,0:T(8,128)(2,1)} %param.8) | copy-start | bytes 1966084
  66.4 20.2 %all-to-all-start.4 = ((bf16[128,20,128]{0,2,1:T(8,128)(2,1)}), bf16[128,20,128]{0,2,1:T(8,128)(2,1)S(1)}, u32[]{:S(2)}, u32[]{:S(2)}) async-start(bf16[128,20,128]{0,2,1:T(8,128)(2,1)} %bitcast.34), calls=%async_computation.4 | async-start | bytes 1310720 | tf_op jit(solution)/shard_map/all_to_all | solution.py:69
  73.3 17.9 %copy-start.32 = (bf16[1,5,4,32,128]{4,3,2,1,0:T(8,128)(2,1)}, bf16[1,5,4,32,128]{4,3,2,1,0:T(8,128)(2,1)S(1)}, u32[]{:S(2)}) copy-start(bf16[1,5,4,32,128]{4,3,2,1,0:T(8,128)(2,1)S(1)} %copy.266) | copy-start | bytes 491524
  73.3 18.3 %copy-start.34 = (bf16[1,5,4,32,128]{4,3,2,1,0:T(8,128)(2,1)}, bf16[1,5,4,32,128]{4,3,2,1,0:T(8,128)(2,1)S(1)}, u32[]{:S(2)}) copy-start(bf16[1,5,4,32,128]{4,3,2,1,0:T(8,128)(2,1)S(1)} %copy.261) | copy-start | bytes 491524
  73.3 19.4 %copy-start.44 = (bf16[1,5,4,32,128]{4,3,2,1,0:T(8,128)(2,1)}, bf16[1,5,4,32,128]{4,3,2,1,0:T(8,128)(2,1)S(1)}, u32[]{:S(2)}) copy-start(bf16[1,5,4,32,128]{4,3,2,1,0:T(8,128)(2,1)S(1)} %copy.271) | copy-start | bytes 491524
  75.8 16.9 %copy-start.8 = (bf16[128,4,5,128]{3,0,1,2:T(8,128)(2,1)}, bf16[128,4,5,128]{3,0,1,2:T(8,128)(2,1)S(1)}, u32[]{:S(2)}) copy-start(bf16[128,4,5,128]{3,0,1,2:T(8,128)(2,1)S(1)} %copy.269) | copy-start | bytes 1966084
  86.7 9.4 %copy-start.6 = (bf16[128,20,128]{0,2,1:T(8,128)(2,1)}, bf16[128,20,128]{0,2,1:T(8,128)(2,1)S(1)}, u32[]{:S(2)}) copy-start(bf16[128,20,128]{0,2,1:T(8,128)(2,1)S(1)} %all-to-all-done.4) | copy-start | bytes 1966084
  86.7 20.2 %all-to-all-start.2 = ((bf16[128,20,128]{0,2,1:T(8,128)(2,1)}), bf16[128,20,128]{0,2,1:T(8,128)(2,1)S(1)}, u32[]{:S(2)}, u32[]{:S(2)}) async-start(bf16[128,20,128]{0,2,1:T(8,128)(2,1)} %bitcast.399), calls=%async_computation.2 | async-start | bytes 1310720 | tf_op jit(solution)/shard_map/all_to_all | solution.py:70
  91.6 3.2 %copy-start.39 = (f32[5,128,4,128]{3,1,2,0:T(8,128)}, f32[5,128,4,128]{3,1,2,0:T(8,128)S(1)}, u32[]{:S(2)}) copy-start(f32[5,128,4,128]{3,1,2,0:T(8,128)S(1)} %fusion.83) | copy-start | bytes 3932164
  92.7 2.1 copy-start.41
  94.8 1.3 copy-start.23
  106.9 21.0 %all-to-all-start.1 = ((bf16[128,20,128]{0,2,1:T(8,128)(2,1)}), bf16[128,20,128]{0,2,1:T(8,128)(2,1)}, u32[]{:S(2)}, u32[]{:S(2)}) async-start(bf16[128,20,128]{0,2,1:T(8,128)(2,1)} %bitcast.398), calls=%async_computation.1 | async-start | bytes 1310720 | tf_op jit(solution)/shard_map/all_to_all | solution.py:71
  114.9 15.2 %copy-start.46 = (bf16[1,5,4,32,128]{4,3,2,1,0:T(8,128)(2,1)S(1)}, bf16[1,5,4,32,128]{4,3,2,1,0:T(8,128)(2,1)}, u32[]{:S(2)}) copy-start(bf16[1,5,4,32,128]{4,3,2,1,0:T(8,128)(2,1)} %copy.245) | copy-start | bytes 491524
  130.1 1.6 copy-start.18
  130.1 1.6 copy-start.47
  134.4 2.7 copy-start
  134.9 2.2 copy-start.2
  140.5 2.2 copy-start.16
  146.3 1.6 copy-start.31
  146.3 1.2 copy-start.13
  148.3 2.3 copy-start.30
  152.8 2.8 copy-start.52
  153.9 1.7 copy-start.36
  153.9 1.3 copy-start.9
  153.9 1.8 copy-start.42
  155.2 1.4 copy-start.40
  156.6 2.1 copy-start.7
  158.7 1.4 copy-start.25
  159.5 1.3 copy-start.3
  159.5 1.7 copy-start.5
  160.1 1.7 copy-start.1
  162.5 5.0 %copy-start.24 = (bf16[4,128,5,128]{1,3,0,2:T(8,128)(2,1)S(1)}, bf16[4,128,5,128]{1,3,0,2:T(8,128)(2,1)}, u32[]{:S(2)}) copy-start(bf16[4,128,5,128]{1,3,0,2:T(8,128)(2,1)} %copy-done.23) | copy-start | bytes 1966084
  163.9 4.7 %copy-start.22 = (bf16[4,128,5,128]{1,3,0,2:T(8,128)(2,1)S(1)}, bf16[4,128,5,128]{1,3,0,2:T(8,128)(2,1)}, u32[]{:S(2)}) copy-start(bf16[4,128,5,128]{1,3,0,2:T(8,128)(2,1)} %copy-done.21) | copy-start | bytes 1966084
  163.9 20.4 %all-to-all-start.8 = ((bf16[3,5,128,128]{3,0,1,2:T(4,128)(2,1)}), bf16[3,5,128,128]{3,0,1,2:T(4,128)(2,1)S(1)}, u32[]{:S(2)}, u32[]{:S(2)}) async-start(bf16[3,5,128,128]{3,0,1,2:T(4,128)(2,1)} %copy.307), calls=%async_computation.8 | async-start | bytes 1310720 | tf_op jit(solution)/shard_map/all_to_all | solution.py:107
  169.7 1.5 copy-start.28
  169.7 1.5 copy-start.35
  184.3 28.7 %all-to-all-start.7 = ((bf16[512,5,128]{2,1,0:T(8,128)(2,1)}), bf16[512,5,128]{2,1,0:T(8,128)(2,1)S(1)}, u32[]{:S(2)}, u32[]{:S(2)}) async-start(bf16[512,5,128]{2,1,0:T(8,128)(2,1)} %copy.298), calls=%async_computation.7 | async-start | bytes 2097152 | tf_op jit(solution)/shard_map/all_to_all | solution.py:103
  187.8 2.7 copy-start.20
  191.6 1.6 copy-start.33
  191.6 1.7 copy-start.38
  213.0 28.7 %all-to-all-start.6 = ((bf16[512,5,128]{2,1,0:T(8,128)(2,1)}), bf16[512,5,128]{2,1,0:T(8,128)(2,1)S(1)}, u32[]{:S(2)}, u32[]{:S(2)}) async-start(bf16[512,5,128]{2,1,0:T(8,128)(2,1)} %copy.293), calls=%async_computation.6 | async-start | bytes 2097152 | tf_op jit(solution)/shard_map/all_to_all | solution.py:102
  216.5 59.7 %all-reduce.5.cloned.1.call-start = ((), (), s32[]{:S(2)}) async-start(), calls=%async_computation.9 | async-start | bytes 983040 | tf_op jit(solution)/shard_map/psum | solution.py:113
  (15 other events, 15.6 us)
Sparse Core Ops, SparseCore 0:
  221.0 55.0 all-reduce.4
where the time goes:
time: 286 us; the launch traced here: 285 us
  waiting for transfers between devices  157 us (55%)
  local copies, waits for them, and re-layouts  38.6 us (13%)
  matrix products  35.5 us (12%)
  starting transfers between devices  35.3 us (12%)
  between operations  14.9 us (5%)
  other arithmetic  4.3 us (2%)
    psum x1, waiting for transfers between devices, local(): lax.psum(state_shard.astype(jnp.bfloat16), 'dp').astype(jnp.float32)  32.8 us
    all_to_all x1, waiting for transfers between devices, local(): lax.all_to_all(d_keys.reshape(back_shape), 'ctx', split_axis=0, concat_ax...  22.5 us
    unnamed x114, local copies, waits for them, and re-layouts  20.4 us
    all_to_all x1, waiting for transfers between devices, local(): lax.all_to_all(d_values.reshape(back_shape), 'ctx', split_axis=0, concat_...  16.7 us
    all_to_all x1, waiting for transfers between devices, local(): lax.all_to_all(padded[0], 'ctx', split_axis=1, concat_axis=0, tiled=True)  15.7 us
    all_to_all x1, waiting for transfers between devices, local(): lax.all_to_all(start_pad, 'ctx', split_axis=1, concat_axis=2, tiled=True)  12.9 us
    all_to_all x1, waiting for transfers between devices, local(): lax.all_to_all(padded[3], 'ctx', split_axis=1, concat_axis=0, tiled=True)  12.7 us
    all_to_all x1, waiting for transfers between devices, local(): lax.all_to_all(next_pad, 'ctx', split_axis=1, concat_axis=2, tiled=True)  12.2 us
  transfers between devices with their start and end apart: 10, of which 10 were waited for; matrix products, arithmetic and copies ran while one was open for 12% of the time, Pallas kernels for 0%

commit v1 on v0

v1 whole, which is shorter than its diff:
```python
import functools

import jax
import jax.numpy as jnp
from jax import lax
from jax.experimental import pallas as pl
from jax.experimental.pallas import tpu as pltpu
from jax.sharding import PartitionSpec as P

RATE = 4.0
CA = 3.4445
CB = -4.775
CC = 2.0315
STEPS = 2
F32 = jnp.float32
BF16 = jnp.bfloat16
VMEM_LIMIT = 48 * 1024 * 1024


def dot_nn(a, b):
    return lax.dot_general(a, b, (((1,), (0,)), ((), ())), preferred_element_type=F32)


def dot_nt(a, b):
    return lax.dot_general(a, b, (((1,), (1,)), ((), ())), preferred_element_type=F32)


def dot_tn(a, b):
    return lax.dot_general(a, b, (((0,), (0,)), ((), ())), preferred_element_type=F32)


def pack_kernel(idx, k_ref, v_ref, q_ref, o_ref, s0_ref, sn_ref, *outs, n, per, heads, chunks):
    tokens = k_ref.shape[1]
    rows = s0_ref.shape[2]
    width = s0_ref.shape[3]
    at = 0
    for first, count in chunks:
        for slot in range(n):
            for j in range(count):
                head = jnp.minimum(idx[slot] * per + first + j, heads - 1)
                cols = pl.ds(pl.multiple_of(head * width, width), width)
                for out, left, right, state in (
                    (outs[at], k_ref, v_ref, s0_ref),
                    (outs[at + 1], q_ref, o_ref, sn_ref),
                ):
                    out[j, 0:tokens, :] = left[0, :, cols]
                    out[j, tokens : 2 * tokens, :] = right[0, :, cols]
                    parts = jnp.concatenate([state[m, head] for m in range(3)], axis=0)
                    out[j, 2 * tokens : 2 * tokens + 3 * rows, :] = parts.astype(BF16)
            at += 2


def swish_terms(g):
    s = 1.0 / (1.0 + jnp.exp(-g))
    sw = g * s
    slope = s * (1.0 + g * (1.0 - s))
    return s, sw, slope


def newton_pullback(grads, updates):
    count = len(grads)
    each = range(count)
    inv = [lax.rsqrt(jnp.sum(g * g, keepdims=True) + 1e-06) for g in grads]
    xs = [[(grads[m] * inv[m]).astype(BF16) for m in each]]
    grams = []
    polys = []
    for step in range(STEPS):
        x = xs[-1]
        gram = [dot_nt(x[m], x[m]).astype(BF16) for m in each]
        poly = [(CB * gram[m].astype(F32) + CC * dot_nn(gram[m], gram[m])).astype(BF16) for m in each]
        grams.append(gram)
        polys.append(poly)
        if step + 1 < STEPS:
            xs.append([(CA * x[m].astype(F32) + dot_nn(poly[m], x[m])).astype(BF16) for m in each])
    d = updates
    for step in reversed(range(STEPS)):
        x, gram, poly = xs[step], grams[step], polys[step]
        dp = [dot_nt(d[m], x[m]) for m in each]
        sym = [dp[m] + dp[m].T for m in each]
        turned = [dot_nn(sym[m].astype(BF16), gram[m]) for m in each]
        da = [(CB * sym[m] + CC * (turned[m] + turned[m].T)).astype(BF16) for m in each]
        d = [
            (CA * d[m].astype(F32) + dot_nn(poly[m], d[m]) + dot_nn(da[m], x[m])).astype(BF16)
            for m in each
        ]
    out = []
    for m in each:
        df = d[m].astype(F32)
        along = jnp.sum(df * grads[m], keepdims=True)
        out.append(df * inv[m] - grads[m] * (along * (inv[m] * inv[m] * inv[m])))
    return out


def chunk_kernel(idx, *refs, n, count, rows):
    a_refs, b_refs = refs[:n], refs[n : 2 * n]
    d_refs, c_ref = refs[2 * n : 3 * n], refs[3 * n]
    w0, w1, gsum, ssum, acts, fields = refs[3 * n + 1 :]
    tokens = (a_refs[0].shape[1] - 3 * rows) // 2
    width = a_refs[0].shape[2]
    for slot in range(n):
        at = pl.multiple_of(idx[slot] * rows, rows)
        for j in range(count):
            for dst, src in ((w0, a_refs[slot]), (w1, b_refs[slot])):
                part = src[j, 2 * tokens : 2 * tokens + 3 * rows, :].astype(F32)
                for m in range(3):
                    dst[3 * j + m, pl.ds(at, rows), :] = part[m * rows : (m + 1) * rows]

    def forward(j, token_refs, w, keep):
        x = jnp.concatenate([r[j, 0:tokens, :] for r in token_refs], axis=0)
        y = jnp.concatenate([r[j, tokens : 2 * tokens, :] for r in token_refs], axis=0)
        wab = jnp.concatenate([w[3 * j], w[3 * j + 1]], axis=1).astype(BF16)
        gu = dot_nn(x, wab)
        g, u = gu[:, :width], gu[:, width:]
        p = dot_nn(y, w[3 * j + 2].astype(BF16))
        s, sw, slope = swish_terms(g)
        hidden = (sw * u).astype(BF16)
        dg = (p * u * slope).astype(BF16)
        du = (p * sw).astype(BF16)
        if keep:
            acts[j, 0], acts[j, 1], acts[j, 2] = g, u, p
            fields[j, 0], fields[j, 1], fields[j, 2] = dg, du, hidden
        ab = dot_tn(x, jnp.concatenate([dg, du], axis=1))
        return ab[:, :width], ab[:, width:], dot_tn(y, hidden)

    for j in range(count):
        for m, val in enumerate(forward(j, a_refs, w0, True)):
            gsum[3 * j + m] = val
        for m, val in enumerate(forward(j, b_refs, w1, False)):
            ssum[3 * j + m] = val

    slots = range(3 * count)
    grads = [gsum[m] for m in slots]
    updates = [(RATE * ssum[m]).astype(BF16) for m in slots]
    for m, val in enumerate(newton_pullback(grads, updates)):
        gsum[m] = val

    for j in range(count):
        x = jnp.concatenate([r[j, 0:tokens, :] for r in a_refs], axis=0)
        y = jnp.concatenate([r[j, tokens : 2 * tokens, :] for r in a_refs], axis=0)
        fab = jnp.concatenate([gsum[3 * j], gsum[3 * j + 1]], axis=1).astype(BF16)
        fc = gsum[3 * j + 2].astype(BF16)
        wab = jnp.concatenate([w0[3 * j], w0[3 * j + 1]], axis=1).astype(BF16)
        wc = w0[3 * j + 2].astype(BF16)
        cdgu = dot_nn(x, fab)
        cdg, cdu = cdgu[:, :width], cdgu[:, width:]
        ch = dot_nn(y, fc)
        g, u, p = acts[j, 0], acts[j, 1], acts[j, 2]
        s, sw, slope = swish_terms(g)
        curve = s * (1.0 - s) * (2.0 + g * (1.0 - 2.0 * s))
        cg = ((ch * u + cdu * p) * slope + cdg * (p * u) * curve).astype(BF16)
        cu = (ch * sw + cdg * p * slope).astype(BF16)
        cp = (cdu * sw + cdg * u * slope).astype(BF16)
        dg, du, hidden = fields[j, 0], fields[j, 1], fields[j, 2]
        dx = dot_nt(jnp.concatenate([dg, du, cg, cu], axis=1), jnp.concatenate([fab, wab], axis=1))
        dy = dot_nt(jnp.concatenate([hidden, cp], axis=1), jnp.concatenate([fc, wc], axis=1))
        for slot in range(n):
            d_refs[slot][j, 0:tokens, :] = dx[slot * tokens : (slot + 1) * tokens].astype(BF16)
            d_refs[slot][j, tokens : 2 * tokens, :] = dy[slot * tokens : (slot + 1) * tokens].astype(BF16)
        ab = dot_tn(x, jnp.concatenate([cg, cu], axis=1))
        c_ref[3 * j] = (ssum[3 * j] + ab[:, :width]).astype(BF16)
        c_ref[3 * j + 1] = (ssum[3 * j + 1] + ab[:, width:]).astype(BF16)
        c_ref[3 * j + 2] = (ssum[3 * j + 2] + dot_tn(y, cp)).astype(BF16)
    for m in range(3 * count, c_ref.shape[0]):
        c_ref[m] = jnp.zeros(c_ref.shape[1:], BF16)


def unpack_kernel(idx, *refs, n, per, heads, chunks):
    ins, (dk, dv) = refs[:-2], refs[-2:]
    tokens = dk.shape[1]
    width = dk.shape[2] // heads
    at = 0
    for first, count in chunks:
        for slot in range(n):
            for j in range(count):
                head = idx[slot] * per + first + j

                @pl.when(head < heads)
                def _(head=head, ref=ins[at], j=j):
                    cols = pl.ds(pl.multiple_of(head * width, width), width)
                    dk[0, :, cols] = ref[j, 0:tokens, :]
                    dv[0, :, cols] = ref[j, tokens : 2 * tokens, :]

            at += 1


def local(keys_a, values_a, queries_b, grad_out, state_start, state_next):
    n = lax.axis_size("ctx")
    n_dp = lax.axis_size("dp")
    tokens = keys_a.shape[1]
    _, heads, rows, width = state_start.shape
    per = -(-heads // n)
    split = max(1, per - 1)
    chunks = [c for c in ((0, split), (split, per - split)) if c[1] > 0]
    me = lax.axis_index("ctx")
    idx = jnp.bitwise_xor(me, jnp.arange(n, dtype=jnp.int32))
    smem = pl.BlockSpec(memory_space=pltpu.SMEM)
    vmem = pl.BlockSpec(memory_space=pltpu.VMEM)
    params = pltpu.CompilerParams(vmem_limit_bytes=VMEM_LIMIT)

    packed_shapes = []
    for _, count in chunks:
        one = jax.ShapeDtypeStruct((count, 2 * tokens + 3 * rows, width), BF16)
        packed_shapes += [one] * (2 * n)
    packed = pl.pallas_call(
        functools.partial(pack_kernel, n=n, per=per, heads=heads, chunks=chunks),
        out_shape=packed_shapes,
        in_specs=[smem] + [vmem] * 6,
        out_specs=[vmem] * len(packed_shapes),
        compiler_params=params,
        name="pack",
    )(idx, keys_a, values_a, queries_b, grad_out, state_start, state_next[0])

    def exchange(value, slot):
        if slot == 0:
            return value
        return lax.ppermute(value, "ctx", [(i, i ^ slot) for i in range(n)])

    back = []
    states = []
    for c, (first, count) in enumerate(chunks):
        sent = packed[2 * n * c : 2 * n * (c + 1)]
        a_in = [exchange(sent[2 * s], s) for s in range(n)]
        b_in = [exchange(sent[2 * s + 1], s) for s in range(n)]
        slots = -(-3 * count // n_dp) * n_dp
        rows_all = n * tokens
        outs = pl.pallas_call(
            functools.partial(chunk_kernel, n=n, count=count, rows=rows),
            out_shape=[jax.ShapeDtypeStruct((count, 2 * tokens, width), BF16)] * n
            + [jax.ShapeDtypeStruct((slots, width, width), BF16)],
            in_specs=[smem] + [vmem] * (2 * n),
            out_specs=[vmem] * (n + 1),
            scratch_shapes=[
                pltpu.VMEM((3 * count, width, width), F32),
                pltpu.VMEM((3 * count, width, width), F32),
                pltpu.VMEM((3 * count, width, width), F32),
                pltpu.VMEM((3 * count, width, width), F32),
                pltpu.VMEM((count, 3, rows_all, width), F32),
                pltpu.VMEM((count, 3, rows_all, width), BF16),
            ],
            compiler_params=params,
            cost_estimate=pl.CostEstimate(
                flops=count * 640 * 10**6, bytes_accessed=count * 10**6, transcendentals=0
            ),
            name=f"chunk{c}",
        )(idx, *a_in, *b_in)
        back += [exchange(outs[s], s) for s in range(n)]
        states.append((first, count, slots, outs[n]))

    grad_keys, grad_values = pl.pallas_call(
        functools.partial(unpack_kernel, n=n, per=per, heads=heads, chunks=chunks),
        out_shape=[
            jax.ShapeDtypeStruct(keys_a.shape, BF16),
            jax.ShapeDtypeStruct(values_a.shape, BF16),
        ],
        in_specs=[smem] + [vmem] * len(back),
        out_specs=[vmem] * 2,
        compiler_params=params,
        name="unpack",
    )(idx, *back)

    pieces = []
    for first, count, slots, state in states:
        own = slots // n_dp
        spread = lax.all_to_all(
            state.reshape(n_dp, own, width, width), "dp", split_axis=0, concat_axis=0, tiled=True
        )
        summed = jnp.sum(spread.astype(F32), axis=0).astype(BF16)
        by_rows = summed.reshape(own, n, rows, width).transpose(1, 0, 2, 3)
        turned = lax.all_to_all(by_rows, "ctx", split_axis=0, concat_axis=0, tiled=True)
        copies = jnp.broadcast_to(turned[None], (n_dp,) + turned.shape)
        full = lax.all_to_all(copies, "dp", split_axis=0, concat_axis=0, tiled=True)
        full = full.transpose(1, 0, 2, 3, 4).reshape(n, slots, rows, width)[:, : 3 * count]
        pieces.append(full.reshape(n, count, 3, rows, width))
    whole = jnp.concatenate(pieces, axis=1).reshape(n * per, 3, rows, width)[:heads]
    grad_state = whole.transpose(1, 0, 2, 3).astype(F32) / n_dp
    return grad_keys, grad_values, grad_state


def solution(mesh):
    placed = (
        P("dp", "ctx", None),
        P("dp", "ctx", None),
        P("dp", "ctx", None),
        P("dp", "ctx", None),
        P(None, None, "ctx", None),
        P("dp", None, None, "ctx", None),
    )
    return jax.shard_map(
        local,
        mesh=mesh,
        in_specs=placed,
        out_specs=(P("dp", "ctx", None), P("dp", "ctx", None), P(None, None, "ctx", None)),
        check_vma=False,
    )
```

time: 286 us -> 178 us (0.62)
  waiting for transfers between devices: 157 us -> 73.4 us
  blocking collectives: 0 us -> 38.5 us
  matrix products: 35.5 us -> 0 us
  local copies, waits for them, and re-layouts: 38.6 us -> 6.03 us
  Pallas kernels: 0 us -> 16.1 us
  between operations: 14.9 us -> 0.79 us
  starting transfers between devices: 35.3 us -> 40.4 us
    all_to_all x9 -> x3, waiting for transfers between devices: 124 us -> 6.77 us  [the longest x2 6.77 us: local(): full = lax.all_to_all(copies, 'dp', split_axis=0, concat_axis=0, tiled=True)]
    ppermute x0 -> x18, waiting for transfers between devices: none -> 66.6 us  [exchange(): return lax.ppermute(value, 'ctx', [(i, i ^ slot) for i in range(n)])]
    all_to_all x0 -> x3, blocking collectives: none -> 38.5 us  [the longest x2 23.8 us: local(): lax.all_to_all(state.reshape(n_dp, own, width, width), 'dp', split_axis=0...]
    psum x1 -> x0, waiting for transfers between devices: 32.8 us -> none  [local(): lax.psum(state_shard.astype(jnp.bfloat16), 'dp').astype(jnp.float32)]
    ppermute x0 -> x18, starting transfers between devices: none -> 30.1 us  [exchange(): return lax.ppermute(value, 'ctx', [(i, i ^ slot) for i in range(n)])]
    dot_general x37 -> x0, matrix products: 29.7 us -> none  [the longest x5 5.95 us: newton(): jnp.einsum('mde,mef->mdf', poly_term, iterate, preferred_element_type=jnp...]
    all_to_all x9 -> x3, starting transfers between devices: 35.2 us -> 10.3 us  [the longest x2 7.04 us: local(): full = lax.all_to_all(copies, 'dp', split_axis=0, concat_axis=0, tiled=True)]
    unnamed x114 -> x10, local copies, waits for them, and re-layouts: 20.4 us -> 3.27 us
  transfers between devices with their start and end apart: 10 -> 21, of which waited for: 10 -> 6; matrix products, arithmetic and copies ran while one was open for 12% -> 1% of each run, Pallas kernels for 0% -> 8%
where the time goes in v1:
time: 178 us; the launch traced here: 177 us
  waiting for transfers between devices  73.4 us (41%)
  starting transfers between devices  40.4 us (23%)
  blocking collectives  38.5 us (22%)
  Pallas kernels  16.1 us (9%)
  local copies, waits for them, and re-layouts  6.03 us (3%)
  other arithmetic  1.81 us (1%)
    ppermute x18, waiting for transfers between devices, exchange(): return lax.ppermute(value, 'ctx', [(i, i ^ slot) for i in range(n)])  66.6 us
    ppermute x18, starting transfers between devices, exchange(): return lax.ppermute(value, 'ctx', [(i, i ^ slot) for i in range(n)])  30.1 us
    all_to_all x2, blocking collectives, local(): lax.all_to_all(state.reshape(n_dp, own, width, width), 'dp', split_axis=0...  23.8 us
    all_to_all x1, blocking collectives, local(): lax.all_to_all(by_rows, 'ctx', split_axis=0, concat_axis=0, tiled=True)  14.7 us
    pallas_call x2, Pallas kernels, local(): pl.pallas_call(functools.partial(chunk_kernel, n=n, count=count, rows=row...  11.8 us
    all_to_all x2, starting transfers between devices, local(): full = lax.all_to_all(copies, 'dp', split_axis=0, concat_axis=0, tiled=True)  7.04 us
    all_to_all x2, waiting for transfers between devices, local(): full = lax.all_to_all(copies, 'dp', split_axis=0, concat_axis=0, tiled=True)  6.77 us
  transfers between devices with their start and end apart: 21, of which 6 were waited for; matrix products, arithmetic and copies ran while one was open for 1% of the time, Pallas kernels for 8%

profile of v1, /device:TPU:0, one launch (start us, length us, event | category | flops | bytes accessed | tf_op | source)
XLA Modules:
  0.0 177.0 jit_solution(2816905047390895026)
XLA Ops:
  0.6 0.0 copy-start
  0.7 1.1 copy-done
  1.7 1.1 copy-done.1
  2.8 1.1 copy-done.2
  3.9 2.3 %pack.1 = (bf16[4,352,128]{2,1,0:T(8,128)(2,1)S(1)}, bf16[4,352,128]{2,1,0:T(8,128)(2,1)S(1)}, bf16[4,352,128]{2,1,0:T(8,128)(2,1)S(1)}, bf16[4,352,128]{2,1,0:T...) custom-call(s32[4]{0:T(128)S(1)} %iota_xor_fusion.idx, ...), custom_call_target="tpu_custom_call" | custom-call | tf_op jit(solution)/shard_map/pack/pallas_call | solution.py:204
  6.2 3.1 %collective-permute-start = (bf16[4,352,128]{2,1,0:T(8,128)(2,1)S(1)}, bf16[4,352,128]{2,1,0:T(8,128)(2,1)S(1)}, u32[]{:S(2)}, u32[]{:S(2)}) collective-permute-start(bf16[4,352,128]{2,1,0:T(8,128)(2,1)S(1)} %get-tuple-element.32), channel_id=1, source_target_pairs={{0,1},{1,0},{2,3},{3,2},{4,5},{5,4},{6,7},{7,6},{8,9},{9,8},{10,11... | collective-permute-start | bytes 1081352 | tf_op jit(solution)/shard_map/ppermute | solution.py:216
  9.3 0.1 collective-permute-start.9
  9.3 3.0 %collective-permute-start.10 = (bf16[1,352,128]{2,1,0:T(8,128)(2,1)S(1)}, bf16[1,352,128]{2,1,0:T(8,128)(2,1)S(1)}, u32[]{:S(2)}, u32[]{:S(2)}) collective-permute-start(bf16[1,352,128]{2,1,0:T(8,128)(2,1)S(1)} %get-tuple-element.45), channel_id=1, source_target_pairs={{0,2},{1,3},{2,0},{3,1},{4,6},{5,7},{6,4},{7,5},{8,10},{9,11},{10,... | collective-permute-start | bytes 270344 | tf_op jit(solution)/shard_map/ppermute | solution.py:216
  12.3 1.3 collective-permute-start.11
  13.7 0.2 collective-permute-start.12
  13.9 8.5 %collective-permute-done.9.refs_1_ = bf16[1,352,128]{2,1,0:T(8,128)(2,1)S(1)} collective-permute-done((bf16[1,352,128]{2,1,0:T(8,128)(2,1)S(1)}, bf16[1,352,128]{2,1,0:T(8,128)(2,1)S(1)}, u32[]{:S(2)}, u32[]{:S(2)}) %collective-permute-start.9) | collective-permute-done | bytes 90144 | tf_op jit(solution)/shard_map/ppermute | solution.py:216
  22.4 3.8 %collective-permute-start.13 = (bf16[1,352,128]{2,1,0:T(8,128)(2,1)S(1)}, bf16[1,352,128]{2,1,0:T(8,128)(2,1)S(1)}, u32[]{:S(2)}, u32[]{:S(2)}) collective-permute-start(bf16[1,352,128]{2,1,0:T(8,128)(2,1)S(1)} %get-tuple-element.49), channel_id=1, source_target_pairs={{0,2},{1,3},{2,0},{3,1},{4,6},{5,7},{6,4},{7,5},{8,10},{9,11},{10,... | collective-permute-start | bytes 270344 | tf_op jit(solution)/shard_map/ppermute | solution.py:216
  26.2 2.0 %collective-permute-start.14 = (bf16[1,352,128]{2,1,0:T(8,128)(2,1)S(1)}, bf16[1,352,128]{2,1,0:T(8,128)(2,1)S(1)}, u32[]{:S(2)}, u32[]{:S(2)}) collective-permute-start(bf16[1,352,128]{2,1,0:T(8,128)(2,1)S(1)} %get-tuple-element.50), channel_id=1, source_target_pairs={{0,3},{1,2},{2,1},{3,0},{4,7},{5,6},{6,5},{7,4},{8,11},{9,10},{10,... | collective-permute-start | bytes 270344 | tf_op jit(solution)/shard_map/ppermute | solution.py:216
  28.2 2.0 %collective-permute-start.1 = (bf16[4,352,128]{2,1,0:T(8,128)(2,1)S(1)}, bf16[4,352,128]{2,1,0:T(8,128)(2,1)S(1)}, u32[]{:S(2)}, u32[]{:S(2)}) collective-permute-start(bf16[4,352,128]{2,1,0:T(8,128)(2,1)S(1)} %get-tuple-element.33), channel_id=1, source_target_pairs={{0,2},{1,3},{2,0},{3,1},{4,6},{5,7},{6,4},{7,5},{8,10},{9,11},{10,... | collective-permute-start | bytes 1081352 | tf_op jit(solution)/shard_map/ppermute | solution.py:216
  30.2 1.0 collective-permute-start.2
  31.2 16.4 %collective-permute-done.13.refs_6_ = bf16[1,352,128]{2,1,0:T(8,128)(2,1)S(1)} collective-permute-done((bf16[1,352,128]{2,1,0:T(8,128)(2,1)S(1)}, bf16[1,352,128]{2,1,0:T(8,128)(2,1)S(1)}, u32[]{:S(2)}, u32[]{:S(2)}) %collective-permute-start.13) | collective-permute-done | bytes 90144 | tf_op jit(solution)/shard_map/ppermute | solution.py:216
  47.5 0.0 collective-permute-done.14.refs_7_
  47.5 3.8 %collective-permute-start.4 = (bf16[4,352,128]{2,1,0:T(8,128)(2,1)S(1)}, bf16[4,352,128]{2,1,0:T(8,128)(2,1)}, u32[]{:S(2)}, u32[]{:S(2)}) collective-permute-start(bf16[4,352,128]{2,1,0:T(8,128)(2,1)S(1)} %get-tuple-element.37), channel_id=1, source_target_pairs={{0,2},{1,3},{2,0},{3,1},{4,6},{5,7},{6,4},{7,5},{8,10},{9,11},{10,... | collective-permute-start | bytes 1081352 | tf_op jit(solution)/shard_map/ppermute | solution.py:216
  51.3 1.8 %collective-permute-start.5 = (bf16[4,352,128]{2,1,0:T(8,128)(2,1)S(1)}, bf16[4,352,128]{2,1,0:T(8,128)(2,1)}, u32[]{:S(2)}, u32[]{:S(2)}) collective-permute-start(bf16[4,352,128]{2,1,0:T(8,128)(2,1)S(1)} %get-tuple-element.38), channel_id=1, source_target_pairs={{0,3},{1,2},{2,1},{3,0},{4,7},{5,6},{6,5},{7,4},{8,11},{9,10},{10,... | collective-permute-start | bytes 1081352 | tf_op jit(solution)/shard_map/ppermute | solution.py:216
  53.2 3.7 %chunk1.1 = (bf16[1,256,128]{2,1,0:T(8,128)(2,1)S(1)}, bf16[1,256,128]{2,1,0:T(8,128)(2,1)S(1)}, bf16[1,256,128]{2,1,0:T(8,128)(2,1)S(1)}, bf16[1,256,128]{2,1,0:T(8,128)(2,1)S(1)}, bf16[8,128,128]{2,1,0:T(8,128)(2,1)S(1)}) custom-call(s32[4]{0:T(128)S(1)} %iota_xor_fusion.idx, bf16[1,352,128]{2,1,0:T(8,128)(2,1)S(1)} %get-tuple-element.43.refs_0_, ...), custom_call_target="tpu_custom_call" | custom-call | flops 640000000 | bytes 1000000 | tf_op jit(solution)/shard_map/chunk1/pallas_call | solution.py:226
  56.9 0.0 copy-start.3
  56.9 10.6 %all_to_all.30 = bf16[8,1,128,128]{3,2,1,0:T(8,128)(2,1)} all-to-all(bf16[8,1,128,128]{3,2,1,0:T(8,128)(2,1)S(1)} %bitcast.27), channel_id=1, replica_groups=mesh['dp'=8,'ctx'=4] {'dp'}, dimensions={0} | all-to-all | bytes 524288 | tf_op jit(solution)/shard_map/all_to_all | solution.py:264
  67.4 1.6 reduce_sum.25
  69.1 3.3 %all-to-all-start.4 = ((bf16[4,1,32,128]{3,2,1,0:T(8,128)(2,1)}), bf16[4,1,32,128]{3,2,1,0:T(8,128)(2,1)S(1)}, u32[]{:S(2)}, u32[]{:S(2)}) async-start(bf16[4,1,32,128]{3,2,1,0:T(8,128)(2,1)} %bitcast.9), calls=%async_computation.4 | async-start | bytes 65536 | tf_op jit(solution)/shard_map/all_to_all | solution.py:269
  72.3 1.1 collective-permute-done.1.refs_2_
  73.4 0.0 collective-permute-done.2.refs_3_
  73.4 0.0 collective-permute-done.3.refs_5_
  73.4 15.9 %collective-permute-done.4.refs_6_ = bf16[4,352,128]{2,1,0:T(8,128)(2,1)} collective-permute-done((bf16[4,352,128]{2,1,0:T(8,128)(2,1)S(1)}, bf16[4,352,128]{2,1,0:T(8,128)(2,1)}, u32[]{:S(2)}, u32[]{:S(2)}) %collective-permute-start.4) | collective-permute-done | bytes 360480 | tf_op jit(solution)/shard_map/ppermute | solution.py:216
  89.3 8.1 %chunk0.1 = (bf16[4,256,128]{2,1,0:T(8,128)(2,1)S(1)}, bf16[4,256,128]{2,1,0:T(8,128)(2,1)S(1)}, bf16[4,256,128]{2,1,0:T(8,128)(2,1)S(1)}, bf16[4,256,128]{2,1,0:T(8,128)(2,1)S(1)}, bf16[16,128,128]{2,1,0:T(8,128)(2,1)S(1)}) custom-call(s32[4]{0:T(128)S(1)} %iota_xor_fusion.idx, bf16[4,352,128]{2,1,0:T(8,128)(2,1)S(1)} %get-tuple-element.31.refs_0_, ...), custom_call_target="tpu_custom_call" | custom-call | flops 2560000000 | bytes 4000000 | tf_op jit(solution)/shard_map/chunk0/pallas_call | solution.py:226
  97.5 0.0 all-to-all-done.4
  97.5 13.3 %all_to_all.31 = bf16[8,2,128,128]{3,2,1,0:T(8,128)(2,1)S(1)} all-to-all(bf16[8,2,128,128]{3,2,1,0:T(8,128)(2,1)S(1)} %bitcast.26), channel_id=1, replica_groups=mesh['dp'=8,'ctx'=4] {'dp'}, dimensions={0} | all-to-all | bytes 1048576 | tf_op jit(solution)/shard_map/all_to_all | solution.py:264
  110.7 0.7 broadcast_in_dim.16
  111.5 3.4 %all-to-all-start.5 = ((bf16[8,4,1,32,128]{4,3,1,2,0:T(8,128)(2,1)}), bf16[8,4,1,32,128]{4,3,1,2,0:T(8,128)(2,1)S(1)}, u32[]{:S(2)}, u32[]{:S(2)}) async-start(bf16[8,4,1,32,128]{4,3,1,2,0:T(8,128)(2,1)} %broadcast_in_dim.16), calls=%async_computation.5 | async-start | bytes 524288 | tf_op jit(solution)/shard_map/all_to_all | solution.py:271
  114.9 0.1 reduce_sum.24
  115.0 6.8 %all-to-all-done.5 = bf16[8,4,1,32,128]{4,3,1,2,0:T(8,128)(2,1)S(1)} async-done(((bf16[8,4,1,32,128]{4,3,1,2,0:T(8,128)(2,1)}), bf16[8,4,1,32,128]{4,3,1,2,0:T(8,128)(2,1)S(1)}, u32[]{:S(2)}, u32[]{:S(2)}) %all-to-all-start.5) | async-done | bytes 262176 | tf_op jit(solution)/shard_map/all_to_all | solution.py:271
  121.8 14.7 %all_to_all.32 = bf16[4,2,32,128]{3,2,1,0:T(8,128)(2,1)S(1)} all-to-all(bf16[4,2,32,128]{3,2,1,0:T(8,128)(2,1)S(1)} %copy.13), channel_id=1, replica_groups=mesh['dp'=8,'ctx'=4] {'ctx'}, dimensions={0} | all-to-all | bytes 131072 | tf_op jit(solution)/shard_map/all_to_all | solution.py:269
  136.5 0.9 broadcast_in_dim.6
  137.4 3.6 %all-to-all-start.2 = ((bf16[8,4,2,32,128]{4,3,2,1,0:T(8,128)(2,1)}), bf16[8,4,2,32,128]{4,3,2,1,0:T(8,128)(2,1)S(1)}, u32[]{:S(2)}, u32[]{:S(2)}) async-start(bf16[8,4,2,32,128]{4,3,2,1,0:T(8,128)(2,1)} %broadcast_in_dim.6), calls=%async_computation.2 | async-start | bytes 1048576 | tf_op jit(solution)/shard_map/all_to_all | solution.py:271
  141.0 1.0 collective-permute-start.15
  142.0 1.1 collective-permute-start.6
  143.1 0.7 collective-permute-start.7
  143.9 2.5 %collective-permute-start.8 = (bf16[4,256,128]{2,1,0:T(8,128)(2,1)S(1)}, bf16[4,256,128]{2,1,0:T(8,128)(2,1)S(1)}, u32[]{:S(2)}, u32[]{:S(2)}) collective-permute-start(bf16[4,256,128]{2,1,0:T(8,128)(2,1)S(1)} %get-tuple-element.42), channel_id=1, source_target_pairs={{0,3},{1,2},{2,1},{3,0},{4,7},{5,6},{6,5},{7,4},{8,11},{9,10},{10,... | collective-permute-start | bytes 786440 | tf_op jit(solution)/shard_map/ppermute | solution.py:216
  146.4 0.0 collective-permute-done.15.refs_5_
  146.5 2.6 %collective-permute-start.17 = (bf16[1,256,128]{2,1,0:T(8,128)(2,1)S(1)}, bf16[1,256,128]{2,1,0:T(8,128)(2,1)S(1)}, u32[]{:S(2)}, u32[]{:S(2)}) collective-permute-start(bf16[1,256,128]{2,1,0:T(8,128)(2,1)S(1)} %get-tuple-element.54), channel_id=1, source_target_pairs={{0,3},{1,2},{2,1},{3,0},{4,7},{5,6},{6,5},{7,4},{8,11},{9,10},{10,... | collective-permute-start | bytes 196616 | tf_op jit(solution)/shard_map/ppermute | solution.py:216
  149.1 24.7 %collective-permute-done.16.refs_6_ = bf16[1,256,128]{2,1,0:T(8,128)(2,1)S(1)} collective-permute-done((bf16[1,256,128]{2,1,0:T(8,128)(2,1)S(1)}, bf16[1,256,128]{2,1,0:T(8,128)(2,1)S(1)}, u32[]{:S(2)}, u32[]{:S(2)}) %collective-permute-start.16) | collective-permute-done | bytes 65568 | tf_op jit(solution)/shard_map/ppermute | solution.py:216
  173.9 2.0 %unpack.1 = (bf16[1,128,2560]{2,1,0:T(8,128)(2,1)}, bf16[1,128,2560]{2,1,0:T(8,128)(2,1)}) custom-call(s32[4]{0:T(128)S(1)} %iota_xor_fusion.idx, bf16[4,256,128]{2,1,0:T(8,128)(2,1)S(1)} %get-tuple-element.39.refs_0_, bf16[4,256,128]{2,1,0:T(8,128)(2,1)S(1)} %collective-permute-done.6.refs_1_, bf16[4,256,128]{2,1,0:T(8,128)(2,1)S(1)} %collective-permute-done.7.refs_2_, ...), custom_call_target="tpu_custom_call" | custom-call | tf_op jit(solution)/shard_map/unpack/pallas_call | solution.py:249
  175.9 0.1 convert_multiply_fusion
  176.0 1.0 copy_bitcast_fusion
  (23 shorter events, 0.1 us)
Async XLA Ops:
  0.6 1.1 copy-start
  1.7 1.1 copy-start.1
  2.8 1.1 copy-start.2
  6.2 45.2 %collective-permute-start = (bf16[4,352,128]{2,1,0:T(8,128)(2,1)S(1)}, bf16[4,352,128]{2,1,0:T(8,128)(2,1)S(1)}, u32[]{:S(2)}, u32[]{:S(2)}) collective-permute-start(bf16[4,352,128]{2,1,0:T(8,128)(2,1)S(1)} %get-tuple-element.32), channel_id=1, source_target_pairs={{0,1},{1,0},{2,3},{3,2},{4,5},{5,4},{6,7},{7,6},{8,9},{9,8},{10,11... | collective-permute-start | bytes 1081352 | tf_op jit(solution)/shard_map/ppermute | solution.py:216
  9.3 13.1 %collective-permute-start.9 = (bf16[1,352,128]{2,1,0:T(8,128)(2,1)S(1)}, bf16[1,352,128]{2,1,0:T(8,128)(2,1)S(1)}, u32[]{:S(2)}, u32[]{:S(2)}) collective-permute-start(bf16[1,352,128]{2,1,0:T(8,128)(2,1)S(1)} %get-tuple-element.44), channel_id=1, source_target_pairs={{0,1},{1,0},{2,3},{3,2},{4,5},{5,4},{6,7},{7,6},{8,9},{9,8},{10,11... | collective-permute-start | bytes 270344 | tf_op jit(solution)/shard_map/ppermute | solution.py:216
  9.3 16.8 %collective-permute-start.10 = (bf16[1,352,128]{2,1,0:T(8,128)(2,1)S(1)}, bf16[1,352,128]{2,1,0:T(8,128)(2,1)S(1)}, u32[]{:S(2)}, u32[]{:S(2)}) collective-permute-start(bf16[1,352,128]{2,1,0:T(8,128)(2,1)S(1)} %get-tuple-element.45), channel_id=1, source_target_pairs={{0,2},{1,3},{2,0},{3,1},{4,6},{5,7},{6,4},{7,5},{8,10},{9,11},{10,... | collective-permute-start | bytes 270344 | tf_op jit(solution)/shard_map/ppermute | solution.py:216
  12.3 15.8 %collective-permute-start.11 = (bf16[1,352,128]{2,1,0:T(8,128)(2,1)S(1)}, bf16[1,352,128]{2,1,0:T(8,128)(2,1)S(1)}, u32[]{:S(2)}, u32[]{:S(2)}) collective-permute-start(bf16[1,352,128]{2,1,0:T(8,128)(2,1)S(1)} %get-tuple-element.46), channel_id=1, source_target_pairs={{0,3},{1,2},{2,1},{3,0},{4,7},{5,6},{6,5},{7,4},{8,11},{9,10},{10,... | collective-permute-start | bytes 270344 | tf_op jit(solution)/shard_map/ppermute | solution.py:216
  13.7 16.5 %collective-permute-start.12 = (bf16[1,352,128]{2,1,0:T(8,128)(2,1)S(1)}, bf16[1,352,128]{2,1,0:T(8,128)(2,1)S(1)}, u32[]{:S(2)}, u32[]{:S(2)}) collective-permute-start(bf16[1,352,128]{2,1,0:T(8,128)(2,1)S(1)} %get-tuple-element.48), channel_id=1, source_target_pairs={{0,1},{1,0},{2,3},{3,2},{4,5},{5,4},{6,7},{7,6},{8,9},{9,8},{10,11... | collective-permute-start | bytes 270344 | tf_op jit(solution)/shard_map/ppermute | solution.py:216
  22.4 25.2 %collective-permute-start.13 = (bf16[1,352,128]{2,1,0:T(8,128)(2,1)S(1)}, bf16[1,352,128]{2,1,0:T(8,128)(2,1)S(1)}, u32[]{:S(2)}, u32[]{:S(2)}) collective-permute-start(bf16[1,352,128]{2,1,0:T(8,128)(2,1)S(1)} %get-tuple-element.49), channel_id=1, source_target_pairs={{0,2},{1,3},{2,0},{3,1},{4,6},{5,7},{6,4},{7,5},{8,10},{9,11},{10,... | collective-permute-start | bytes 270344 | tf_op jit(solution)/shard_map/ppermute | solution.py:216
  26.2 21.4 %collective-permute-start.14 = (bf16[1,352,128]{2,1,0:T(8,128)(2,1)S(1)}, bf16[1,352,128]{2,1,0:T(8,128)(2,1)S(1)}, u32[]{:S(2)}, u32[]{:S(2)}) collective-permute-start(bf16[1,352,128]{2,1,0:T(8,128)(2,1)S(1)} %get-tuple-element.50), channel_id=1, source_target_pairs={{0,3},{1,2},{2,1},{3,0},{4,7},{5,6},{6,5},{7,4},{8,11},{9,10},{10,... | collective-permute-start | bytes 270344 | tf_op jit(solution)/shard_map/ppermute | solution.py:216
  28.2 45.2 %collective-permute-start.1 = (bf16[4,352,128]{2,1,0:T(8,128)(2,1)S(1)}, bf16[4,352,128]{2,1,0:T(8,128)(2,1)S(1)}, u32[]{:S(2)}, u32[]{:S(2)}) collective-permute-start(bf16[4,352,128]{2,1,0:T(8,128)(2,1)S(1)} %get-tuple-element.33), channel_id=1, source_target_pairs={{0,2},{1,3},{2,0},{3,1},{4,6},{5,7},{6,4},{7,5},{8,10},{9,11},{10,... | collective-permute-start | bytes 1081352 | tf_op jit(solution)/shard_map/ppermute | solution.py:216
  30.2 43.2 %collective-permute-start.2 = (bf16[4,352,128]{2,1,0:T(8,128)(2,1)S(1)}, bf16[4,352,128]{2,1,0:T(8,128)(2,1)}, u32[]{:S(2)}, u32[]{:S(2)}) collective-permute-start(bf16[4,352,128]{2,1,0:T(8,128)(2,1)S(1)} %get-tuple-element.34), channel_id=1, source_target_pairs={{0,3},{1,2},{2,1},{3,0},{4,7},{5,6},{6,5},{7,4},{8,11},{9,10},{10,... | collective-permute-start | bytes 1081352 | tf_op jit(solution)/shard_map/ppermute | solution.py:216
  47.5 25.9 %collective-permute-start.3 = (bf16[4,352,128]{2,1,0:T(8,128)(2,1)S(1)}, bf16[4,352,128]{2,1,0:T(8,128)(2,1)}, u32[]{:S(2)}, u32[]{:S(2)}) collective-permute-start(bf16[4,352,128]{2,1,0:T(8,128)(2,1)S(1)} %get-tuple-element.36), channel_id=1, source_target_pairs={{0,1},{1,0},{2,3},{3,2},{4,5},{5,4},{6,7},{7,6},{8,9},{9,8},{10,11... | collective-permute-start | bytes 1081352 | tf_op jit(solution)/shard_map/ppermute | solution.py:216
  47.5 41.8 %collective-permute-start.4 = (bf16[4,352,128]{2,1,0:T(8,128)(2,1)S(1)}, bf16[4,352,128]{2,1,0:T(8,128)(2,1)}, u32[]{:S(2)}, u32[]{:S(2)}) collective-permute-start(bf16[4,352,128]{2,1,0:T(8,128)(2,1)S(1)} %get-tuple-element.37), channel_id=1, source_target_pairs={{0,2},{1,3},{2,0},{3,1},{4,6},{5,7},{6,4},{7,5},{8,10},{9,11},{10,... | collective-permute-start | bytes 1081352 | tf_op jit(solution)/shard_map/ppermute | solution.py:216
  51.3 38.0 %collective-permute-start.5 = (bf16[4,352,128]{2,1,0:T(8,128)(2,1)S(1)}, bf16[4,352,128]{2,1,0:T(8,128)(2,1)}, u32[]{:S(2)}, u32[]{:S(2)}) collective-permute-start(bf16[4,352,128]{2,1,0:T(8,128)(2,1)S(1)} %get-tuple-element.38), channel_id=1, source_target_pairs={{0,3},{1,2},{2,1},{3,0},{4,7},{5,6},{6,5},{7,4},{8,11},{9,10},{10,... | collective-permute-start | bytes 1081352 | tf_op jit(solution)/shard_map/ppermute | solution.py:216
  56.9 10.6 %copy-start.3 = (bf16[1,256,128]{2,1,0:T(8,128)(2,1)}, bf16[1,256,128]{2,1,0:T(8,128)(2,1)S(1)}, u32[]{:S(2)}) copy-start(bf16[1,256,128]{2,1,0:T(8,128)(2,1)S(1)} %get-tuple-element.52) | copy-start | bytes 196612
  69.1 28.4 %all-to-all-start.4 = ((bf16[4,1,32,128]{3,2,1,0:T(8,128)(2,1)}), bf16[4,1,32,128]{3,2,1,0:T(8,128)(2,1)S(1)}, u32[]{:S(2)}, u32[]{:S(2)}) async-start(bf16[4,1,32,128]{3,2,1,0:T(8,128)(2,1)} %bitcast.9), calls=%async_computation.4 | async-start | bytes 65536 | tf_op jit(solution)/shard_map/all_to_all | solution.py:269
  111.5 10.3 %all-to-all-start.5 = ((bf16[8,4,1,32,128]{4,3,1,2,0:T(8,128)(2,1)}), bf16[8,4,1,32,128]{4,3,1,2,0:T(8,128)(2,1)S(1)}, u32[]{:S(2)}, u32[]{:S(2)}) async-start(bf16[8,4,1,32,128]{4,3,1,2,0:T(8,128)(2,1)} %broadcast_in_dim.16), calls=%async_computation.5 | async-start | bytes 524288 | tf_op jit(solution)/shard_map/all_to_all | solution.py:271
  137.4 3.6 %copy-start.4 = (bf16[1,256,128]{2,1,0:T(8,128)(2,1)S(1)}, bf16[1,256,128]{2,1,0:T(8,128)(2,1)}, u32[]{:S(2)}) copy-start(bf16[1,256,128]{2,1,0:T(8,128)(2,1)} %copy-done.3) | copy-start | bytes 196612
  137.4 38.4 %all-to-all-start.2 = ((bf16[8,4,2,32,128]{4,3,2,1,0:T(8,128)(2,1)}), bf16[8,4,2,32,128]{4,3,2,1,0:T(8,128)(2,1)S(1)}, u32[]{:S(2)}, u32[]{:S(2)}) async-start(bf16[8,4,2,32,128]{4,3,2,1,0:T(8,128)(2,1)} %broadcast_in_dim.6), calls=%async_computation.2 | async-start | bytes 1048576 | tf_op jit(solution)/shard_map/all_to_all | solution.py:271
  141.0 5.4 %collective-permute-start.15 = (bf16[1,256,128]{2,1,0:T(8,128)(2,1)S(1)}, bf16[1,256,128]{2,1,0:T(8,128)(2,1)S(1)}, u32[]{:S(2)}, u32[]{:S(2)}) collective-permute-start(bf16[1,256,128]{2,1,0:T(8,128)(2,1)S(1)} %copy-done.4), channel_id=1, source_target_pairs={{0,1},{1,0},{2,3},{3,2},{4,5},{5,4},{6,7},{7,6},{8,9},{9,8},{10,11... | collective-permute-start | bytes 196616 | tf_op jit(solution)/shard_map/ppermute | solution.py:216
  142.0 31.8 %collective-permute-start.6 = (bf16[4,256,128]{2,1,0:T(8,128)(2,1)S(1)}, bf16[4,256,128]{2,1,0:T(8,128)(2,1)S(1)}, u32[]{:S(2)}, u32[]{:S(2)}) collective-permute-start(bf16[4,256,128]{2,1,0:T(8,128)(2,1)S(1)} %get-tuple-element.40), channel_id=1, source_target_pairs={{0,1},{1,0},{2,3},{3,2},{4,5},{5,4},{6,7},{7,6},{8,9},{9,8},{10,11... | collective-permute-start | bytes 786440 | tf_op jit(solution)/shard_map/ppermute | solution.py:216
  143.1 30.7 %collective-permute-start.7 = (bf16[4,256,128]{2,1,0:T(8,128)(2,1)S(1)}, bf16[4,256,128]{2,1,0:T(8,128)(2,1)S(1)}, u32[]{:S(2)}, u32[]{:S(2)}) collective-permute-start(bf16[4,256,128]{2,1,0:T(8,128)(2,1)S(1)} %get-tuple-element.41), channel_id=1, source_target_pairs={{0,2},{1,3},{2,0},{3,1},{4,6},{5,7},{6,4},{7,5},{8,10},{9,11},{10,... | collective-permute-start | bytes 786440 | tf_op jit(solution)/shard_map/ppermute | solution.py:216
  143.9 30.0 %collective-permute-start.8 = (bf16[4,256,128]{2,1,0:T(8,128)(2,1)S(1)}, bf16[4,256,128]{2,1,0:T(8,128)(2,1)S(1)}, u32[]{:S(2)}, u32[]{:S(2)}) collective-permute-start(bf16[4,256,128]{2,1,0:T(8,128)(2,1)S(1)} %get-tuple-element.42), channel_id=1, source_target_pairs={{0,3},{1,2},{2,1},{3,0},{4,7},{5,6},{6,5},{7,4},{8,11},{9,10},{10,... | collective-permute-start | bytes 786440 | tf_op jit(solution)/shard_map/ppermute | solution.py:216
  146.4 27.4 %collective-permute-start.16 = (bf16[1,256,128]{2,1,0:T(8,128)(2,1)S(1)}, bf16[1,256,128]{2,1,0:T(8,128)(2,1)S(1)}, u32[]{:S(2)}, u32[]{:S(2)}) collective-permute-start(bf16[1,256,128]{2,1,0:T(8,128)(2,1)S(1)} %get-tuple-element.53), channel_id=1, source_target_pairs={{0,2},{1,3},{2,0},{3,1},{4,6},{5,7},{6,4},{7,5},{8,10},{9,11},{10,... | collective-permute-start | bytes 196616 | tf_op jit(solution)/shard_map/ppermute | solution.py:216
  146.5 27.4 %collective-permute-start.17 = (bf16[1,256,128]{2,1,0:T(8,128)(2,1)S(1)}, bf16[1,256,128]{2,1,0:T(8,128)(2,1)S(1)}, u32[]{:S(2)}, u32[]{:S(2)}) collective-permute-start(bf16[1,256,128]{2,1,0:T(8,128)(2,1)S(1)} %get-tuple-element.54), channel_id=1, source_target_pairs={{0,3},{1,2},{2,1},{3,0},{4,7},{5,6},{6,5},{7,4},{8,11},{9,10},{10,... | collective-permute-start | bytes 196616 | tf_op jit(solution)/shard_map/ppermute | solution.py:216

commit v2 on v1

v2 whole, which is shorter than its diff:
```python
import functools

import jax
import jax.numpy as jnp
from jax import lax
from jax.experimental import pallas as pl
from jax.experimental.pallas import tpu as pltpu
from jax.sharding import PartitionSpec as P

RATE = 4.0
CA = 3.4445
CB = -4.775
CC = 2.0315
STEPS = 2
F32 = jnp.float32
BF16 = jnp.bfloat16
VMEM_LIMIT = 48 * 1024 * 1024
SMEM = pl.BlockSpec(memory_space=pltpu.SMEM)
VMEM = pl.BlockSpec(memory_space=pltpu.VMEM)
ANY = pl.BlockSpec(memory_space=pl.ANY)


def dot_nn(a, b):
    return lax.dot_general(a, b, (((1,), (0,)), ((), ())), preferred_element_type=F32)


def dot_nt(a, b):
    return lax.dot_general(a, b, (((1,), (1,)), ((), ())), preferred_element_type=F32)


def dot_tn(a, b):
    return lax.dot_general(a, b, (((0,), (0,)), ((), ())), preferred_element_type=F32)


def call(kernel, out_shape, args, in_specs, out_specs, name, scratch=(), flops=10**6, size=10**6):
    return pl.pallas_call(
        kernel,
        out_shape=out_shape,
        in_specs=in_specs,
        out_specs=out_specs,
        scratch_shapes=list(scratch),
        compiler_params=pltpu.CompilerParams(vmem_limit_bytes=VMEM_LIMIT),
        cost_estimate=pl.CostEstimate(flops=flops, bytes_accessed=size, transcendentals=0),
        name=name,
    )(*args)


def swish_terms(g):
    s = 1.0 / (1.0 + jnp.exp(-g))
    sw = g * s
    slope = s * (1.0 + g * (1.0 - s))
    return s, sw, slope


def newton_pullback(grads, updates):
    each = range(len(grads))
    inv = [lax.rsqrt(jnp.sum(g * g, keepdims=True) + 1e-06) for g in grads]
    xs = [[(grads[m] * inv[m]).astype(BF16) for m in each]]
    grams = []
    polys = []
    for step in range(STEPS):
        x = xs[-1]
        gram = [dot_nt(x[m], x[m]).astype(BF16) for m in each]
        poly = [(CB * gram[m].astype(F32) + CC * dot_nn(gram[m], gram[m])).astype(BF16) for m in each]
        grams.append(gram)
        polys.append(poly)
        if step + 1 < STEPS:
            xs.append([(CA * x[m].astype(F32) + dot_nn(poly[m], x[m])).astype(BF16) for m in each])
    d = updates
    for step in reversed(range(STEPS)):
        x, gram, poly = xs[step], grams[step], polys[step]
        dp = [dot_nt(d[m], x[m]) for m in each]
        sym = [dp[m] + dp[m].T for m in each]
        turned = [dot_nn(sym[m].astype(BF16), gram[m]) for m in each]
        da = [(CB * sym[m] + CC * (turned[m] + turned[m].T)).astype(BF16) for m in each]
        d = [
            (CA * d[m].astype(F32) + dot_nn(poly[m], d[m]) + dot_nn(da[m], x[m])).astype(BF16)
            for m in each
        ]
    out = []
    for m in each:
        df = d[m].astype(F32)
        along = jnp.sum(df * grads[m], keepdims=True)
        out.append(df * inv[m] - grads[m] * (along * (inv[m] * inv[m] * inv[m])))
    return out


class Plan:
    def __init__(self, n, n_dp, tokens, heads, rows, width, chunks_of):
        self.n, self.n_dp = n, n_dp
        self.tokens, self.heads, self.rows, self.width = tokens, heads, rows, width
        self.per = -(-heads // n)
        self.mats = 3 * self.per
        self.group = min(4, n_dp)
        self.share = -(-self.mats // self.group)
        self.own = -(-self.mats // n_dp)
        self.block = -(-rows // 16) * 16
        self.share_rows = -(-self.share // self.per) * self.block
        self.chunks = chunks_of(self.per)

    def first_head(self, c):
        return min(c * self.per, self.heads - self.per)


def pack_a_kernel(slot_ref, head_ref, dp_ref, k_ref, v_ref, s_ref, *refs, plan):
    n, t, w, per = plan.n, plan.tokens, plan.width, plan.per
    outs, (state, sems) = refs[:n], refs[n:]
    copies = [pltpu.make_async_copy(s_ref, state, sems.at[2 * n])]
    copies[0].start()
    for slot in range(n):
        cols = pl.ds(pl.multiple_of(head_ref[slot] * w, w), per * w)
        for part, src in enumerate((k_ref, v_ref)):
            copy = pltpu.make_async_copy(
                src.at[0, :, cols], outs[slot].at[pl.ds(part * t, t), :], sems.at[2 * slot + part]
            )
            copy.start()
            copies.append(copy)
    copies[0].wait()
    low = dp_ref[0] % plan.group
    for slot in range(n):
        for q in range(plan.share):
            mat = jnp.minimum(low * plan.share + q, plan.mats - 1)
            part = state[mat % 3, head_ref[slot] + mat // 3].astype(BF16)
            top = 2 * t + (q // per) * plan.block
            left = (q % per) * w
            outs[slot][top : top + plan.rows, left : left + w] = part
    for copy in copies[1:]:
        copy.wait()


def pack_b_kernel(slot_ref, head_ref, q_ref, o_ref, s_ref, *refs, plan):
    n, t, w = plan.n, plan.tokens, plan.width
    chunks = plan.chunks
    outs, (state, sems) = refs[: n * len(chunks)], refs[n * len(chunks) :]
    copies = [pltpu.make_async_copy(s_ref, state, sems.at[2 * n * len(chunks)])]
    copies[0].start()
    for c, (first, count) in enumerate(chunks):
        for slot in range(n):
            at = c * n + slot
            cols = pl.ds(pl.multiple_of((head_ref[slot] + first) * w, w), count * w)
            for part, src in enumerate((q_ref, o_ref)):
                copy = pltpu.make_async_copy(
                    src.at[0, :, cols], outs[at].at[pl.ds(part * t, t), :], sems.at[2 * at + part]
                )
                copy.start()
                copies.append(copy)
    copies[0].wait()
    for c, (first, count) in enumerate(chunks):
        for slot in range(n):
            for j in range(count):
                for m in range(3):
                    part = state[0, m, head_ref[slot] + first + j].astype(BF16)
                    top = 2 * t + m * plan.block
                    outs[c * n + slot][top : top + plan.rows, j * w : (j + 1) * w] = part
    for copy in copies[1:]:
        copy.wait()


def start_kernel(slot_ref, *refs, plan):
    n, w = plan.n, plan.width
    a_refs, (out, whole) = refs[:n], refs[n:]
    for slot in range(n):
        at = pl.ds(pl.multiple_of(slot_ref[slot] * plan.rows, plan.rows), plan.rows)
        for q in range(plan.share):
            top = 2 * plan.tokens + (q // plan.per) * plan.block
            left = (q % plan.per) * w
            whole[q, at, :] = a_refs[slot][top : top + plan.rows, left : left + w].astype(F32)
    out[...] = whole[...].astype(BF16)


def chunk_kernel(slot_ref, dp_ref, *refs, plan, chunk, last):
    n, t, w = plan.n, plan.tokens, plan.width
    first, count = plan.chunks[chunk]
    refs = list(refs)

    def take(k):
        got = refs[:k]
        del refs[:k]
        return got

    a_refs, b_refs, shares = take(n), take(n), take(plan.group)
    before = take(chunk) if last else []
    (d_ref,) = take(1)
    c_refs = take(plan.n_dp if last else 1)
    w0, w1, gsum, ssum, acts, fields = take(6)
    total = take(1)[0] if last else c_refs[0]
    base = 3 * first if last else 0

    low = dp_ref[0] % plan.group
    for k in range(plan.group):
        at = pl.ds(jnp.bitwise_xor(low, k) * plan.share, plan.share)
        w0[at] = shares[k][...]
    for slot in range(n):
        at = pl.ds(pl.multiple_of(slot_ref[slot] * plan.rows, plan.rows), plan.rows)
        for j in range(count):
            for m in range(3):
                top = 2 * t + m * plan.block
                part = b_refs[slot][top : top + plan.rows, j * w : (j + 1) * w]
                w1[3 * j + m, at, :] = part.astype(F32)

    def tokens_of(slots, j):
        cols = slice(j * w, (j + 1) * w)
        x = jnp.concatenate([r[0:t, cols] for r in slots], axis=0)
        y = jnp.concatenate([r[t : 2 * t, cols] for r in slots], axis=0)
        return x, y

    def forward(x, y, wa, wb, wc, keep):
        gu = dot_nn(x, jnp.concatenate([wa, wb], axis=1))
        g, u = gu[:, :w], gu[:, w:]
        p = dot_nn(y, wc)
        _, sw, slope = swish_terms(g)
        hidden = (sw * u).astype(BF16)
        dg = (p * u * slope).astype(BF16)
        du = (p * sw).astype(BF16)
        if keep is not None:
            acts[keep, 0], acts[keep, 1], acts[keep, 2] = g, u, p
            fields[keep, 0], fields[keep, 1], fields[keep, 2] = dg, du, hidden
        ab = dot_tn(x, jnp.concatenate([dg, du], axis=1))
        return ab[:, :w], ab[:, w:], dot_tn(y, hidden)

    for j in range(count):
        x, y = tokens_of(a_refs, first + j)
        at = 3 * (first + j)
        for m, val in enumerate(forward(x, y, w0[at], w0[at + 1], w0[at + 2], j)):
            gsum[3 * j + m] = val
        x, y = tokens_of(b_refs, j)
        weights = [w1[3 * j + m].astype(BF16) for m in range(3)]
        for m, val in enumerate(forward(x, y, *weights, None)):
            ssum[3 * j + m] = val

    mats = range(3 * count)
    grads = [gsum[m] for m in mats]
    updates = [(RATE * ssum[m]).astype(BF16) for m in mats]
    for m, val in enumerate(newton_pullback(grads, updates)):
        gsum[m] = val

    for j in range(count):
        x, y = tokens_of(a_refs, first + j)
        at = 3 * (first + j)
        fab = jnp.concatenate([gsum[3 * j], gsum[3 * j + 1]], axis=1).astype(BF16)
        fc = gsum[3 * j + 2].astype(BF16)
        wab = jnp.concatenate([w0[at], w0[at + 1]], axis=1)
        wc = w0[at + 2]
        cdgu = dot_nn(x, fab)
        cdg, cdu = cdgu[:, :w], cdgu[:, w:]
        ch = dot_nn(y, fc)
        g, u, p = acts[j, 0], acts[j, 1], acts[j, 2]
        s, sw, slope = swish_terms(g)
        curve = s * (1.0 - s) * (2.0 + g * (1.0 - 2.0 * s))
        cg = ((ch * u + cdu * p) * slope + cdg * (p * u) * curve).astype(BF16)
        cu = (ch * sw + cdg * p * slope).astype(BF16)
        cp = (cdu * sw + cdg * u * slope).astype(BF16)
        dg, du, hidden = fields[j, 0], fields[j, 1], fields[j, 2]
        dx = dot_nt(jnp.concatenate([dg, du, cg, cu], axis=1), jnp.concatenate([fab, wab], axis=1))
        dy = dot_nt(jnp.concatenate([hidden, cp], axis=1), jnp.concatenate([fc, wc], axis=1))
        cols = slice(j * w, (j + 1) * w)
        for slot in range(n):
            to = slot_ref[slot]
            d_ref[to, 0:t, cols] = dx[slot * t : (slot + 1) * t].astype(BF16)
            d_ref[to, t : 2 * t, cols] = dy[slot * t : (slot + 1) * t].astype(BF16)
        ab = dot_tn(x, jnp.concatenate([cg, cu], axis=1))
        grown = (ab[:, :w], ab[:, w:], dot_tn(y, cp))
        for m in range(3):
            total[base + 3 * j + m] = (ssum[3 * j + m] + grown[m]).astype(BF16)

    if last:
        for c, part in enumerate(before):
            at = 3 * plan.chunks[c][0]
            total[at : at + part.shape[0]] = part[...]
        for m in range(plan.mats, plan.n_dp * plan.own):
            total[m] = jnp.zeros((w, w), BF16)
        for k in range(plan.n_dp):
            at = jnp.bitwise_xor(dp_ref[0], k) * plan.own
            c_refs[k][...] = total[pl.ds(at, plan.own)]


def sum_kernel(slot_ref, *refs, plan):
    parts, outs, whole = refs[: plan.n_dp], refs[plan.n_dp : -1], refs[-1]
    added = parts[0][...].astype(F32)
    for part in parts[1:]:
        added = added + part[...].astype(F32)
    whole[...] = added / plan.n_dp
    for slot in range(plan.n):
        at = pl.ds(pl.multiple_of(slot_ref[slot] * plan.rows, plan.rows), plan.rows)
        outs[slot][...] = whole[:, at, :].astype(BF16)


def order_kernel(slot_ref, *refs, plan):
    for slot in range(plan.n):
        refs[-1][slot_ref[slot]] = refs[slot][...]


def state_kernel(dp_ref, *refs, plan):
    out = refs[-1]
    for k in range(plan.n_dp):
        for i in range(plan.own):
            mat = jnp.bitwise_xor(dp_ref[0], k) * plan.own + i

            @pl.when(mat < plan.mats)
            def _(mat=mat, ref=refs[k], i=i):
                for c in range(plan.n):
                    out[mat % 3, plan.first_head(c) + mat // 3] = ref[c, i].astype(F32)


def unpack_kernel(*refs, plan):
    chunks = plan.chunks
    t, w = plan.tokens, plan.width
    ins, (dk, dv, sems) = refs[: len(chunks)], refs[len(chunks) :]
    copies = []
    for c, (first, count) in enumerate(chunks):
        for owner in range(plan.n):
            cols = pl.ds((plan.first_head(owner) + first) * w, count * w)
            for part, dst in enumerate((dk, dv)):
                copy = pltpu.make_async_copy(
                    ins[c].at[owner, pl.ds(part * t, t), :],
                    dst.at[0, :, cols],
                    sems.at[(c * plan.n + owner) * 2 + part],
                )
                copy.start()
                copies.append(copy)
        if plan.n * plan.per != plan.heads:
            for copy in copies:
                copy.wait()
            copies = []
    for copy in copies:
        copy.wait()


def chunks_of(per):
    split = (per + 1) // 2
    return [c for c in ((0, split), (split, per - split)) if c[1] > 0]


def local(keys_a, values_a, queries_b, grad_out, state_start, state_next):
    n, n_dp = lax.axis_size("ctx"), lax.axis_size("dp")
    _, heads, rows, width = state_start.shape
    t = keys_a.shape[1]
    plan = Plan(n, n_dp, t, heads, rows, width, chunks_of)
    per, chunks = plan.per, plan.chunks
    bind = lambda kernel, **more: functools.partial(kernel, plan=plan, **more)

    slot_ids = jnp.bitwise_xor(lax.axis_index("ctx"), jnp.arange(n, dtype=jnp.int32))
    head_ids = jnp.minimum(slot_ids * per, heads - per)
    dp_id = lax.axis_index("dp").reshape(1)

    def swap(value, axis, size, k):
        if k == 0:
            return value
        return lax.ppermute(value, axis, [(i, i ^ k) for i in range(size)])

    def shape(*dims, dtype=BF16):
        return jax.ShapeDtypeStruct(dims, dtype)

    a_sent = call(
        bind(pack_a_kernel),
        [shape(2 * t + plan.share_rows, per * width)] * n,
        (slot_ids, head_ids, dp_id, keys_a, values_a, state_start),
        [SMEM] * 3 + [ANY] * 3,
        [VMEM] * n,
        "pack_a",
        [pltpu.VMEM(state_start.shape, F32), pltpu.SemaphoreType.DMA((2 * n + 1,))],
    )
    a_in = [swap(a_sent[s], "ctx", n, s) for s in range(n)]
    b_sent = call(
        bind(pack_b_kernel),
        [shape(2 * t + 3 * plan.block, count * width) for _, count in chunks for _ in range(n)],
        (slot_ids, head_ids, queries_b, grad_out, state_next),
        [SMEM] * 2 + [ANY] * 3,
        [VMEM] * (n * len(chunks)),
        "pack_b",
        [pltpu.VMEM(state_next.shape, F32), pltpu.SemaphoreType.DMA((2 * n * len(chunks) + 1,))],
    )
    b_in = [
        [swap(b_sent[c * n + s], "ctx", n, s) for s in range(n)] for c in range(len(chunks))
    ]
    start_own = call(
        bind(start_kernel),
        shape(plan.share, width, width),
        (slot_ids, *a_in),
        [SMEM] + [VMEM] * n,
        VMEM,
        "start_share",
        [pltpu.VMEM((plan.share, width, width), F32)],
    )
    shares = [swap(start_own, "dp", n_dp, k) for k in range(plan.group)]

    back = []
    sums = []
    for c, (first, count) in enumerate(chunks):
        last = c + 1 == len(chunks)
        before = sums if last else []
        mats = 3 * count
        if last:
            c_shapes = [shape(plan.own, width, width)] * n_dp
        else:
            c_shapes = [shape(mats, width, width)]
        scratch = [
            pltpu.VMEM((plan.group * plan.share, width, width), BF16),
            pltpu.VMEM((mats, width, width), F32),
            pltpu.VMEM((mats, width, width), F32),
            pltpu.VMEM((mats, width, width), F32),
            pltpu.VMEM((count, 3, n * t, width), F32),
            pltpu.VMEM((count, 3, n * t, width), BF16),
        ]
        if last:
            scratch.append(pltpu.VMEM((n_dp * plan.own, width, width), BF16))
        outs = call(
            bind(chunk_kernel, chunk=c, last=last),
            [shape(n, 2 * t, count * width)] + c_shapes,
            (slot_ids, dp_id, *a_in, *b_in[c], *shares, *before),
            [SMEM] * 2 + [VMEM] * (2 * n + plan.group + len(before)),
            [VMEM] * (1 + len(c_shapes)),
            f"chunk{c}",
            scratch,
            flops=count * 640 * 10**6,
            size=count * 10**6,
        )
        back.append(lax.all_to_all(outs[0], "ctx", split_axis=0, concat_axis=0, tiled=True))
        sums += outs[1:]

    parts = sums[len(chunks) - 1 :]
    parts = [swap(parts[k], "dp", n_dp, k) for k in range(n_dp)]
    by_rows = call(
        bind(sum_kernel),
        [shape(plan.own, rows, width)] * n,
        (slot_ids, *parts),
        [SMEM] + [VMEM] * n_dp,
        [VMEM] * n,
        "state_sum",
        [pltpu.VMEM((plan.own, width, width), F32)],
    )
    by_rows = [swap(by_rows[s], "ctx", n, s) for s in range(n)]
    mine = call(
        bind(order_kernel),
        shape(n, plan.own, rows, width),
        (slot_ids, *by_rows),
        [SMEM] + [VMEM] * n,
        VMEM,
        "state_order",
    )
    everyone = [swap(mine, "dp", n_dp, k) for k in range(n_dp)]
    grad_state = call(
        bind(state_kernel),
        shape(*state_start.shape, dtype=F32),
        (dp_id, *everyone),
        [SMEM] + [VMEM] * n_dp,
        VMEM,
        "state_out",
    )
    grad_keys, grad_values = call(
        bind(unpack_kernel),
        [shape(*keys_a.shape), shape(*values_a.shape)],
        back,
        [VMEM] * len(back),
        [ANY] * 2,
        "unpack",
        [pltpu.SemaphoreType.DMA((2 * n * len(chunks),))],
    )
    return grad_keys, grad_values, grad_state


def solution(mesh):
    placed = (
        P("dp", "ctx", None),
        P("dp", "ctx", None),
        P("dp", "ctx", None),
        P("dp", "ctx", None),
        P(None, None, "ctx", None),
        P("dp", None, None, "ctx", None),
    )
    return jax.shard_map(
        local,
        mesh=mesh,
        in_specs=placed,
        out_specs=(P("dp", "ctx", None), P("dp", "ctx", None), P(None, None, "ctx", None)),
        check_vma=False,
    )
```

time: 178 us -> 141 us (0.79)
  blocking collectives: 38.5 us -> 17.8 us
  waiting for transfers between devices: 73.4 us -> 56.4 us
  starting transfers between devices: 40.4 us -> 43.6 us
  local copies, waits for them, and re-layouts: 6.03 us -> 3.38 us
  Pallas kernels: 16.1 us -> 18.4 us
  other arithmetic: 1.81 us -> 0.01 us
    all_to_all x3 -> x1, blocking collectives: 38.5 us -> 17.8 us  [local(): lax.all_to_all(outs[0], 'ctx', split_axis=0, concat_axis=0, tiled=True)]
    ppermute x18 -> x29, waiting for transfers between devices: 66.6 us -> 56.4 us  [swap(): return lax.ppermute(value, axis, [(i, i ^ k) for i in range(size)])]
    ppermute x18 -> x29, starting transfers between devices: 30.1 us -> 40.2 us  [swap(): return lax.ppermute(value, axis, [(i, i ^ k) for i in range(size)])]
    all_to_all x3 -> x1, starting transfers between devices: 10.3 us -> 3.49 us  [local(): lax.all_to_all(outs[0], 'ctx', split_axis=0, concat_axis=0, tiled=True)]
    all_to_all x3 -> x1, waiting for transfers between devices: 6.77 us -> 0.01 us  [local(): lax.all_to_all(outs[0], 'ctx', split_axis=0, concat_axis=0, tiled=True)]
    pallas_call x4 -> x9, Pallas kernels: 16.1 us -> 18.4 us  [call(): pl.pallas_call(kernel, out_shape=out_shape, in_specs=in_specs, out_specs=...]
  transfers between devices with their start and end apart: 21 -> 30, of which waited for: 6 -> 15; matrix products, arithmetic and copies ran while one was open for 1% -> 0% of each run, Pallas kernels for 8% -> 8%
where the time goes in v2:
time: 141 us; the launch traced here: 140 us
  waiting for transfers between devices  56.4 us (40%)
  starting transfers between devices  43.6 us (31%)
  Pallas kernels  18.4 us (13%)
  blocking collectives  17.8 us (13%)
  local copies, waits for them, and re-layouts  3.38 us (2%)
    ppermute x29, waiting for transfers between devices, swap(): return lax.ppermute(value, axis, [(i, i ^ k) for i in range(size)])  56.4 us
    ppermute x29, starting transfers between devices, swap(): return lax.ppermute(value, axis, [(i, i ^ k) for i in range(size)])  40.2 us
    pallas_call x9, Pallas kernels, call(): pl.pallas_call(kernel, out_shape=out_shape, in_specs=in_specs, out_specs=...  18.4 us
    all_to_all x1, blocking collectives, local(): lax.all_to_all(outs[0], 'ctx', split_axis=0, concat_axis=0, tiled=True)  17.8 us
    all_to_all x1, starting transfers between devices, local(): lax.all_to_all(outs[0], 'ctx', split_axis=0, concat_axis=0, tiled=True)  3.49 us
    unnamed x12, local copies, waits for them, and re-layouts  3.38 us
  transfers between devices with their start and end apart: 30, of which 15 were waited for; matrix products, arithmetic and copies ran while one was open for 0% of the time, Pallas kernels for 8%

profile of v2, /device:TPU:0, one launch (start us, length us, event | category | flops | bytes accessed | tf_op | source)
XLA Modules:
  0.0 140.5 jit_solution(15063288071633547698)
XLA Ops:
  0.7 1.2 copy-done
  1.9 1.1 copy-done.2
  2.9 1.1 copy-done.3
  4.0 1.2 pack_a.1
  5.2 3.1 %collective-permute-start = (bf16[288,640]{1,0:T(8,128)(2,1)S(1)}, bf16[288,640]{1,0:T(8,128)(2,1)S(1)}, u32[]{:S(2)}, u32[]{:S(2)}) collective-permute-start(bf16[288,640]{1,0:T(8,128)(2,1)S(1)} %get-tuple-element.33), channel_id=1, source_target_pairs={{0,1},{1,0},{2,3},{3,2},{4,5},{5,4},{6,7},{7,6},{8,9},{9,8},{10,11... | collective-permute-start | bytes 1105928 | tf_op jit(solution)/shard_map/ppermute | solution.py:349
  8.3 2.6 %collective-permute-start.1 = (bf16[288,640]{1,0:T(8,128)(2,1)S(1)}, bf16[288,640]{1,0:T(8,128)(2,1)S(1)}, u32[]{:S(2)}, u32[]{:S(2)}) collective-permute-start(bf16[288,640]{1,0:T(8,128)(2,1)S(1)} %get-tuple-element.34), channel_id=1, source_target_pairs={{0,2},{1,3},{2,0},{3,1},{4,6},{5,7},{6,4},{7,5},{8,10},{9,11},{10,... | collective-permute-start | bytes 1105928 | tf_op jit(solution)/shard_map/ppermute | solution.py:349
  10.9 1.3 pack_b.1
  12.2 0.9 collective-permute-start.3
  13.1 3.5 %collective-permute-start.4 = (bf16[352,384]{1,0:T(8,128)(2,1)S(1)}, bf16[352,384]{1,0:T(8,128)(2,1)S(1)}, u32[]{:S(2)}, u32[]{:S(2)}) collective-permute-start(bf16[352,384]{1,0:T(8,128)(2,1)S(1)} %get-tuple-element.38), channel_id=1, source_target_pairs={{0,2},{1,3},{2,0},{3,1},{4,6},{5,7},{6,4},{7,5},{8,10},{9,11},{10,... | collective-permute-start | bytes 811016 | tf_op jit(solution)/shard_map/ppermute | solution.py:349
  16.6 8.2 %collective-permute-done.refs_1_ = bf16[288,640]{1,0:T(8,128)(2,1)S(1)} collective-permute-done((bf16[288,640]{1,0:T(8,128)(2,1)S(1)}, bf16[288,640]{1,0:T(8,128)(2,1)S(1)}, u32[]{:S(2)}, u32[]{:S(2)}) %collective-permute-start) | collective-permute-done | bytes 368672 | tf_op jit(solution)/shard_map/ppermute | solution.py:349
  24.8 4.6 %collective-permute-start.5 = (bf16[352,384]{1,0:T(8,128)(2,1)S(1)}, bf16[352,384]{1,0:T(8,128)(2,1)S(1)}, u32[]{:S(2)}, u32[]{:S(2)}) collective-permute-start(bf16[352,384]{1,0:T(8,128)(2,1)S(1)} %get-tuple-element.39), channel_id=1, source_target_pairs={{0,3},{1,2},{2,1},{3,0},{4,7},{5,6},{6,5},{7,4},{8,11},{9,10},{10,... | collective-permute-start | bytes 811016 | tf_op jit(solution)/shard_map/ppermute | solution.py:349
  29.4 7.1 %collective-permute-done.1.refs_2_ = bf16[288,640]{1,0:T(8,128)(2,1)S(1)} collective-permute-done((bf16[288,640]{1,0:T(8,128)(2,1)S(1)}, bf16[288,640]{1,0:T(8,128)(2,1)S(1)}, u32[]{:S(2)}, u32[]{:S(2)}) %collective-permute-start.1) | collective-permute-done | bytes 368672 | tf_op jit(solution)/shard_map/ppermute | solution.py:349
  36.5 0.6 start_share.1.refs_8_
  37.2 1.6 %collective-permute-start.7 = (bf16[4,128,128]{2,1,0:T(8,128)(2,1)S(1)}, bf16[4,128,128]{2,1,0:T(8,128)(2,1)S(1)}, u32[]{:S(2)}, u32[]{:S(2)}) collective-permute-start(bf16[4,128,128]{2,1,0:T(8,128)(2,1)S(1)} %start_share.1.refs_8_), channel_id=1, source_target_pairs={{0,8},{4,12},{8,0},{12,4},{16,24},{20,28},{24,16},{28,20},{1,9},{5... | collective-permute-start | bytes 393224 | tf_op jit(solution)/shard_map/ppermute | solution.py:349
  39.1 22.8 %collective-permute-done.4.refs_6_ = bf16[352,384]{1,0:T(8,128)(2,1)S(1)} collective-permute-done((bf16[352,384]{1,0:T(8,128)(2,1)S(1)}, bf16[352,384]{1,0:T(8,128)(2,1)S(1)}, u32[]{:S(2)}, u32[]{:S(2)}) %collective-permute-start.4) | collective-permute-done | bytes 270368 | tf_op jit(solution)/shard_map/ppermute | solution.py:349
  61.8 5.9 %collective-permute-start.10 = (bf16[352,256]{1,0:T(8,128)(2,1)S(1)}, bf16[352,256]{1,0:T(8,128)(2,1)S(1)}, u32[]{:S(2)}, u32[]{:S(2)}) collective-permute-start(bf16[352,256]{1,0:T(8,128)(2,1)S(1)} %get-tuple-element.43), channel_id=1, source_target_pairs={{0,2},{1,3},{2,0},{3,1},{4,6},{5,7},{6,4},{7,5},{8,10},{9,11},{10,... | collective-permute-start | bytes 540680 | tf_op jit(solution)/shard_map/ppermute | solution.py:349
  67.8 1.3 collective-permute-start.11
  69.1 7.0 %chunk0.1 = (bf16[4,256,384]{2,1,0:T(8,128)(2,1)}, bf16[9,128,128]{2,1,0:T(8,128)(2,1)S(1)}) custom-call(s32[4]{0:T(128)S(1)} %get-tuple-element.62.slot_ref, s32[1]{0:T(128)} %bitcast.dp_ref, bf16[288,640]{1,0:T(8,128)(2,1)S(1)} %get-tuple-element.32.refs_0_, bf16[288,640]{1,0:T(8,128)(2,1)S(1)} %collective-permute-done.refs_1_, ...), custom_call_target="tpu_custom_call" | custom-call | flops 1920000000 | bytes 3000000 | tf_op jit(solution)/shard_map/chunk0/pallas_call | solution.py:36
  76.2 4.0 %collective-permute-done.10.refs_6_ = bf16[352,256]{1,0:T(8,128)(2,1)S(1)} collective-permute-done((bf16[352,256]{1,0:T(8,128)(2,1)S(1)}, bf16[352,256]{1,0:T(8,128)(2,1)S(1)}, u32[]{:S(2)}, u32[]{:S(2)}) %collective-permute-start.10) | collective-permute-done | bytes 180256 | tf_op jit(solution)/shard_map/ppermute | solution.py:349
  80.1 4.8 %chunk1.1 = (bf16[4,256,256]{2,1,0:T(8,128)(2,1)S(1)}, bf16[2,128,128]{2,1,0:T(8,128)(2,1)S(1)}, bf16[2,128,128]{2,1,0:T(8,128)(2,1)S(1)}, bf16[2,128,128]{2,1,0...) custom-call(s32[4]{0:T(128)S(1)} %get-tuple-element.62.slot_ref, ...), custom_call_target="tpu_custom_call" | custom-call | flops 1280000000 | bytes 2000000 | tf_op jit(solution)/shard_map/chunk1/pallas_call | solution.py:36
  84.9 17.8 %all_to_all.10.refs_1_ = bf16[4,256,256]{2,1,0:T(8,128)(2,1)S(1)} all-to-all(bf16[4,256,256]{2,1,0:T(8,128)(2,1)S(1)} %get-tuple-element.46), channel_id=1, replica_groups=mesh['dp'=8,'ctx'=4] {'ctx'}, dimensions={0} | all-to-all | bytes 1048576 | tf_op jit(solution)/shard_map/all_to_all | solution.py:418
  102.7 3.5 %all-to-all-start = ((bf16[4,256,384]{2,1,0:T(8,128)(2,1)}), bf16[4,256,384]{2,1,0:T(8,128)(2,1)S(1)}, u32[]{:S(2)}, u32[]{:S(2)}) async-start(bf16[4,256,384]{2,1,0:T(8,128)(2,1)} %get-tuple-element.40), calls=%async_computation | async-start | bytes 1572864 | tf_op jit(solution)/shard_map/all_to_all | solution.py:418
  106.3 1.6 %collective-permute-start.13 = (bf16[2,128,128]{2,1,0:T(8,128)(2,1)S(1)}, bf16[2,128,128]{2,1,0:T(8,128)(2,1)S(1)}, u32[]{:S(2)}, u32[]{:S(2)}) collective-permute-start(bf16[2,128,128]{2,1,0:T(8,128)(2,1)S(1)} %get-tuple-element.51), channel_id=1, source_target_pairs={{0,8},{4,12},{8,0},{12,4},{16,24},{20,28},{24,16},{28,20},{1,9},{5... | collective-permute-start | bytes 196616 | tf_op jit(solution)/shard_map/ppermute | solution.py:349
  107.9 0.3 collective-permute-start.14
  108.2 1.5 %collective-permute-start.15 = (bf16[2,128,128]{2,1,0:T(8,128)(2,1)S(1)}, bf16[2,128,128]{2,1,0:T(8,128)(2,1)S(1)}, u32[]{:S(2)}, u32[]{:S(2)}) collective-permute-start(bf16[2,128,128]{2,1,0:T(8,128)(2,1)S(1)} %get-tuple-element.53), channel_id=1, source_target_pairs={{0,16},{4,20},{8,24},{12,28},{16,0},{20,4},{24,8},{28,12},{1,17},{... | collective-permute-start | bytes 196616 | tf_op jit(solution)/shard_map/ppermute | solution.py:349
  109.9 2.5 %collective-permute-start.17 = (bf16[2,128,128]{2,1,0:T(8,128)(2,1)S(1)}, bf16[2,128,128]{2,1,0:T(8,128)(2,1)S(1)}, u32[]{:S(2)}, u32[]{:S(2)}) collective-permute-start(bf16[2,128,128]{2,1,0:T(8,128)(2,1)S(1)} %get-tuple-element.55), channel_id=1, source_target_pairs={{0,24},{4,28},{8,16},{12,20},{16,8},{20,12},{24,0},{28,4},{1,25},{... | collective-permute-start | bytes 196616 | tf_op jit(solution)/shard_map/ppermute | solution.py:349
  112.3 0.2 collective-permute-start.18
  112.6 1.3 collective-permute-done.16.refs_5_
  113.8 1.5 %collective-permute-done.17.refs_6_ = bf16[2,128,128]{2,1,0:T(8,128)(2,1)S(1)} collective-permute-done((bf16[2,128,128]{2,1,0:T(8,128)(2,1)S(1)}, bf16[2,128,128]{2,1,0:T(8,128)(2,1)S(1)}, u32[]{:S(2)}, u32[]{:S(2)}) %collective-permute-start.17) | collective-permute-done | bytes 65568 | tf_op jit(solution)/shard_map/ppermute | solution.py:349
  115.3 2.0 %collective-permute-done.18.refs_7_ = bf16[2,128,128]{2,1,0:T(8,128)(2,1)S(1)} collective-permute-done((bf16[2,128,128]{2,1,0:T(8,128)(2,1)S(1)}, bf16[2,128,128]{2,1,0:T(8,128)(2,1)S(1)}, u32[]{:S(2)}, u32[]{:S(2)}) %collective-permute-start.18) | collective-permute-done | bytes 65568 | tf_op jit(solution)/shard_map/ppermute | solution.py:349
  117.3 0.6 state_sum.1
  117.9 1.9 %collective-permute-start.19 = (bf16[2,32,128]{2,1,0:T(8,128)(2,1)S(1)}, bf16[2,32,128]{2,1,0:T(8,128)(2,1)S(1)}, u32[]{:S(2)}, u32[]{:S(2)}) collective-permute-start(bf16[2,32,128]{2,1,0:T(8,128)(2,1)S(1)} %get-tuple-element.58), channel_id=1, source_target_pairs={{0,1},{1,0},{2,3},{3,2},{4,5},{5,4},{6,7},{7,6},{8,9},{9,8},{10,11... | collective-permute-start | bytes 49160 | tf_op jit(solution)/shard_map/ppermute | solution.py:349
  119.8 2.4 %collective-permute-start.20 = (bf16[2,32,128]{2,1,0:T(8,128)(2,1)S(1)}, bf16[2,32,128]{2,1,0:T(8,128)(2,1)S(1)}, u32[]{:S(2)}, u32[]{:S(2)}) collective-permute-start(bf16[2,32,128]{2,1,0:T(8,128)(2,1)S(1)} %get-tuple-element.59), channel_id=1, source_target_pairs={{0,2},{1,3},{2,0},{3,1},{4,6},{5,7},{6,4},{7,5},{8,10},{9,11},{10,... | collective-permute-start | bytes 49160 | tf_op jit(solution)/shard_map/ppermute | solution.py:349
  122.4 4.1 %collective-permute-done.20.refs_2_ = bf16[2,32,128]{2,1,0:T(8,128)(2,1)S(1)} collective-permute-done((bf16[2,32,128]{2,1,0:T(8,128)(2,1)S(1)}, bf16[2,32,128]{2,1,0:T(8,128)(2,1)S(1)}, u32[]{:S(2)}, u32[]{:S(2)}) %collective-permute-start.20) | collective-permute-done | bytes 16416 | tf_op jit(solution)/shard_map/ppermute | solution.py:349
  126.5 1.3 collective-permute-done.21.refs_3_
  127.7 0.5 state_order.1.refs_0_
  128.4 1.8 %collective-permute-start.27 = (bf16[4,2,32,128]{3,2,1,0:T(8,128)(2,1)S(1)}, bf16[4,2,32,128]{3,2,1,0:T(8,128)(2,1)S(1)}, u32[]{:S(2)}, u32[]{:S(2)}) collective-permute-start(bf16[4,2,32,128]{3,2,1,0:T(8,128)(2,1)S(1)} %state_order.1.refs_0_), channel_id=1, source_target_pairs={{0,24},{4,28},{8,16},{12,20},{16,8},{20,12},{24,0},{28,4},{1,25},{... | collective-permute-start | bytes 196616 | tf_op jit(solution)/shard_map/ppermute | solution.py:349
  130.2 1.2 collective-permute-start.26
  131.4 1.4 collective-permute-start.25
  132.8 0.5 collective-permute-done.28.refs_7_
  133.2 0.5 collective-permute-start.23
  133.7 0.2 collective-permute-done.27.refs_6_
  133.9 0.7 collective-permute-start.22
  134.6 1.1 collective-permute-done.26.refs_5_
  135.8 1.5 %collective-permute-done.25.refs_4_ = bf16[4,2,32,128]{3,2,1,0:T(8,128)(2,1)S(1)} collective-permute-done((bf16[4,2,32,128]{3,2,1,0:T(8,128)(2,1)S(1)}, bf16[4,2,32,128]{3,2,1,0:T(8,128)(2,1)S(1)}, u32[]{:S(2)}, u32[]{:S(2)}) %collective-permute-start.25) | collective-permute-done | bytes 65568 | tf_op jit(solution)/shard_map/ppermute | solution.py:349
  137.3 0.8 collective-permute-done.23.refs_2_
  138.0 1.3 state_out.1
  139.3 1.2 unpack.1
  (35 shorter events, 0.9 us)
Async XLA Ops:
  0.6 1.2 copy-start
  1.9 1.1 copy-start.2
  2.9 1.1 copy-start.3
  4.0 6.9 %copy-start.1 = (f32[1,3,20,32,128]{4,3,2,1,0:T(8,128)S(1)}, f32[1,3,20,32,128]{4,3,2,1,0:T(8,128)}, u32[]{:S(2)}) copy-start(f32[1,3,20,32,128]{4,3,2,1,0:T(8,128)} %s_ref.3) | copy-start | bytes 2949124
  4.0 6.9 %copy-start.4 = (bf16[1,128,2560]{2,1,0:T(8,128)(2,1)S(1)}, bf16[1,128,2560]{2,1,0:T(8,128)(2,1)}, u32[]{:S(2)}) copy-start(bf16[1,128,2560]{2,1,0:T(8,128)(2,1)} %q_ref.1) | copy-start | bytes 1966084
  4.0 6.9 %copy-start.5 = (bf16[1,128,2560]{2,1,0:T(8,128)(2,1)S(1)}, bf16[1,128,2560]{2,1,0:T(8,128)(2,1)}, u32[]{:S(2)}) copy-start(bf16[1,128,2560]{2,1,0:T(8,128)(2,1)} %o_ref.1) | copy-start | bytes 1966084
  5.2 19.6 %collective-permute-start = (bf16[288,640]{1,0:T(8,128)(2,1)S(1)}, bf16[288,640]{1,0:T(8,128)(2,1)S(1)}, u32[]{:S(2)}, u32[]{:S(2)}) collective-permute-start(bf16[288,640]{1,0:T(8,128)(2,1)S(1)} %get-tuple-element.33), channel_id=1, source_target_pairs={{0,1},{1,0},{2,3},{3,2},{4,5},{5,4},{6,7},{7,6},{8,9},{9,8},{10,11... | collective-permute-start | bytes 1105928 | tf_op jit(solution)/shard_map/ppermute | solution.py:349
  8.3 28.3 %collective-permute-start.1 = (bf16[288,640]{1,0:T(8,128)(2,1)S(1)}, bf16[288,640]{1,0:T(8,128)(2,1)S(1)}, u32[]{:S(2)}, u32[]{:S(2)}) collective-permute-start(bf16[288,640]{1,0:T(8,128)(2,1)S(1)} %get-tuple-element.34), channel_id=1, source_target_pairs={{0,2},{1,3},{2,0},{3,1},{4,6},{5,7},{6,4},{7,5},{8,10},{9,11},{10,... | collective-permute-start | bytes 1105928 | tf_op jit(solution)/shard_map/ppermute | solution.py:349
  10.9 25.7 %collective-permute-start.2 = (bf16[288,640]{1,0:T(8,128)(2,1)S(1)}, bf16[288,640]{1,0:T(8,128)(2,1)S(1)}, u32[]{:S(2)}, u32[]{:S(2)}) collective-permute-start(bf16[288,640]{1,0:T(8,128)(2,1)S(1)} %get-tuple-element.35), channel_id=1, source_target_pairs={{0,3},{1,2},{2,1},{3,0},{4,7},{5,6},{6,5},{7,4},{8,11},{9,10},{10,... | collective-permute-start | bytes 1105928 | tf_op jit(solution)/shard_map/ppermute | solution.py:349
  12.2 26.8 %collective-permute-start.3 = (bf16[352,384]{1,0:T(8,128)(2,1)S(1)}, bf16[352,384]{1,0:T(8,128)(2,1)S(1)}, u32[]{:S(2)}, u32[]{:S(2)}) collective-permute-start(bf16[352,384]{1,0:T(8,128)(2,1)S(1)} %get-tuple-element.37), channel_id=1, source_target_pairs={{0,1},{1,0},{2,3},{3,2},{4,5},{5,4},{6,7},{7,6},{8,9},{9,8},{10,11... | collective-permute-start | bytes 811016 | tf_op jit(solution)/shard_map/ppermute | solution.py:349
  13.1 48.7 %collective-permute-start.4 = (bf16[352,384]{1,0:T(8,128)(2,1)S(1)}, bf16[352,384]{1,0:T(8,128)(2,1)S(1)}, u32[]{:S(2)}, u32[]{:S(2)}) collective-permute-start(bf16[352,384]{1,0:T(8,128)(2,1)S(1)} %get-tuple-element.38), channel_id=1, source_target_pairs={{0,2},{1,3},{2,0},{3,1},{4,6},{5,7},{6,4},{7,5},{8,10},{9,11},{10,... | collective-permute-start | bytes 811016 | tf_op jit(solution)/shard_map/ppermute | solution.py:349
  24.8 37.0 %collective-permute-start.5 = (bf16[352,384]{1,0:T(8,128)(2,1)S(1)}, bf16[352,384]{1,0:T(8,128)(2,1)S(1)}, u32[]{:S(2)}, u32[]{:S(2)}) collective-permute-start(bf16[352,384]{1,0:T(8,128)(2,1)S(1)} %get-tuple-element.39), channel_id=1, source_target_pairs={{0,3},{1,2},{2,1},{3,0},{4,7},{5,6},{6,5},{7,4},{8,11},{9,10},{10,... | collective-permute-start | bytes 811016 | tf_op jit(solution)/shard_map/ppermute | solution.py:349
  37.1 30.6 %collective-permute-start.8 = (bf16[4,128,128]{2,1,0:T(8,128)(2,1)S(1)}, bf16[4,128,128]{2,1,0:T(8,128)(2,1)S(1)}, u32[]{:S(2)}, u32[]{:S(2)}) collective-permute-start(bf16[4,128,128]{2,1,0:T(8,128)(2,1)S(1)} %start_share.1.refs_8_), channel_id=1, source_target_pairs={{0,12},{4,8},{8,4},{12,0},{16,28},{20,24},{24,20},{28,16},{1,13},{... | collective-permute-start | bytes 393224 | tf_op jit(solution)/shard_map/ppermute | solution.py:349
  37.2 31.9 %collective-permute-start.7 = (bf16[4,128,128]{2,1,0:T(8,128)(2,1)S(1)}, bf16[4,128,128]{2,1,0:T(8,128)(2,1)S(1)}, u32[]{:S(2)}, u32[]{:S(2)}) collective-permute-start(bf16[4,128,128]{2,1,0:T(8,128)(2,1)S(1)} %start_share.1.refs_8_), channel_id=1, source_target_pairs={{0,8},{4,12},{8,0},{12,4},{16,24},{20,28},{24,16},{28,20},{1,9},{5... | collective-permute-start | bytes 393224 | tf_op jit(solution)/shard_map/ppermute | solution.py:349
  39.0 30.2 %collective-permute-start.6 = (bf16[4,128,128]{2,1,0:T(8,128)(2,1)S(1)}, bf16[4,128,128]{2,1,0:T(8,128)(2,1)S(1)}, u32[]{:S(2)}, u32[]{:S(2)}) collective-permute-start(bf16[4,128,128]{2,1,0:T(8,128)(2,1)S(1)} %start_share.1.refs_8_), channel_id=1, source_target_pairs={{0,4},{4,0},{8,12},{12,8},{16,20},{20,16},{24,28},{28,24},{1,5},{5... | collective-permute-start | bytes 393224 | tf_op jit(solution)/shard_map/ppermute | solution.py:349
  61.8 14.3 %collective-permute-start.9 = (bf16[352,256]{1,0:T(8,128)(2,1)S(1)}, bf16[352,256]{1,0:T(8,128)(2,1)S(1)}, u32[]{:S(2)}, u32[]{:S(2)}) collective-permute-start(bf16[352,256]{1,0:T(8,128)(2,1)S(1)} %get-tuple-element.42), channel_id=1, source_target_pairs={{0,1},{1,0},{2,3},{3,2},{4,5},{5,4},{6,7},{7,6},{8,9},{9,8},{10,11... | collective-permute-start | bytes 540680 | tf_op jit(solution)/shard_map/ppermute | solution.py:349
  61.8 18.3 %collective-permute-start.10 = (bf16[352,256]{1,0:T(8,128)(2,1)S(1)}, bf16[352,256]{1,0:T(8,128)(2,1)S(1)}, u32[]{:S(2)}, u32[]{:S(2)}) collective-permute-start(bf16[352,256]{1,0:T(8,128)(2,1)S(1)} %get-tuple-element.43), channel_id=1, source_target_pairs={{0,2},{1,3},{2,0},{3,1},{4,6},{5,7},{6,4},{7,5},{8,10},{9,11},{10,... | collective-permute-start | bytes 540680 | tf_op jit(solution)/shard_map/ppermute | solution.py:349
  67.8 12.4 %collective-permute-start.11 = (bf16[352,256]{1,0:T(8,128)(2,1)S(1)}, bf16[352,256]{1,0:T(8,128)(2,1)S(1)}, u32[]{:S(2)}, u32[]{:S(2)}) collective-permute-start(bf16[352,256]{1,0:T(8,128)(2,1)S(1)} %get-tuple-element.44), channel_id=1, source_target_pairs={{0,3},{1,2},{2,1},{3,0},{4,7},{5,6},{6,5},{7,4},{8,11},{9,10},{10,... | collective-permute-start | bytes 540680 | tf_op jit(solution)/shard_map/ppermute | solution.py:349
  102.7 36.6 %all-to-all-start = ((bf16[4,256,384]{2,1,0:T(8,128)(2,1)}), bf16[4,256,384]{2,1,0:T(8,128)(2,1)S(1)}, u32[]{:S(2)}, u32[]{:S(2)}) async-start(bf16[4,256,384]{2,1,0:T(8,128)(2,1)} %get-tuple-element.40), calls=%async_computation | async-start | bytes 1572864 | tf_op jit(solution)/shard_map/all_to_all | solution.py:418
  106.2 3.6 %collective-permute-start.12 = (bf16[2,128,128]{2,1,0:T(8,128)(2,1)S(1)}, bf16[2,128,128]{2,1,0:T(8,128)(2,1)S(1)}, u32[]{:S(2)}, u32[]{:S(2)}) collective-permute-start(bf16[2,128,128]{2,1,0:T(8,128)(2,1)S(1)} %get-tuple-element.50), channel_id=1, source_target_pairs={{0,4},{4,0},{8,12},{12,8},{16,20},{20,16},{24,28},{28,24},{1,5},{5... | collective-permute-start | bytes 196616 | tf_op jit(solution)/shard_map/ppermute | solution.py:349
  106.3 6.0 %collective-permute-start.13 = (bf16[2,128,128]{2,1,0:T(8,128)(2,1)S(1)}, bf16[2,128,128]{2,1,0:T(8,128)(2,1)S(1)}, u32[]{:S(2)}, u32[]{:S(2)}) collective-permute-start(bf16[2,128,128]{2,1,0:T(8,128)(2,1)S(1)} %get-tuple-element.51), channel_id=1, source_target_pairs={{0,8},{4,12},{8,0},{12,4},{16,24},{20,28},{24,16},{28,20},{1,9},{5... | collective-permute-start | bytes 196616 | tf_op jit(solution)/shard_map/ppermute | solution.py:349
  107.9 4.7 %collective-permute-start.14 = (bf16[2,128,128]{2,1,0:T(8,128)(2,1)S(1)}, bf16[2,128,128]{2,1,0:T(8,128)(2,1)S(1)}, u32[]{:S(2)}, u32[]{:S(2)}) collective-permute-start(bf16[2,128,128]{2,1,0:T(8,128)(2,1)S(1)} %get-tuple-element.52), channel_id=1, source_target_pairs={{0,12},{4,8},{8,4},{12,0},{16,28},{20,24},{24,20},{28,16},{1,13},{... | collective-permute-start | bytes 196616 | tf_op jit(solution)/shard_map/ppermute | solution.py:349
  108.2 4.4 %collective-permute-start.15 = (bf16[2,128,128]{2,1,0:T(8,128)(2,1)S(1)}, bf16[2,128,128]{2,1,0:T(8,128)(2,1)S(1)}, u32[]{:S(2)}, u32[]{:S(2)}) collective-permute-start(bf16[2,128,128]{2,1,0:T(8,128)(2,1)S(1)} %get-tuple-element.53), channel_id=1, source_target_pairs={{0,16},{4,20},{8,24},{12,28},{16,0},{20,4},{24,8},{28,12},{1,17},{... | collective-permute-start | bytes 196616 | tf_op jit(solution)/shard_map/ppermute | solution.py:349
  109.7 4.2 %collective-permute-start.16 = (bf16[2,128,128]{2,1,0:T(8,128)(2,1)S(1)}, bf16[2,128,128]{2,1,0:T(8,128)(2,1)S(1)}, u32[]{:S(2)}, u32[]{:S(2)}) collective-permute-start(bf16[2,128,128]{2,1,0:T(8,128)(2,1)S(1)} %get-tuple-element.54), channel_id=1, source_target_pairs={{0,20},{4,16},{8,28},{12,24},{16,4},{20,0},{24,12},{28,8},{1,21},{... | collective-permute-start | bytes 196616 | tf_op jit(solution)/shard_map/ppermute | solution.py:349
  109.9 5.5 %collective-permute-start.17 = (bf16[2,128,128]{2,1,0:T(8,128)(2,1)S(1)}, bf16[2,128,128]{2,1,0:T(8,128)(2,1)S(1)}, u32[]{:S(2)}, u32[]{:S(2)}) collective-permute-start(bf16[2,128,128]{2,1,0:T(8,128)(2,1)S(1)} %get-tuple-element.55), channel_id=1, source_target_pairs={{0,24},{4,28},{8,16},{12,20},{16,8},{20,12},{24,0},{28,4},{1,25},{... | collective-permute-start | bytes 196616 | tf_op jit(solution)/shard_map/ppermute | solution.py:349
  112.3 4.9 %collective-permute-start.18 = (bf16[2,128,128]{2,1,0:T(8,128)(2,1)S(1)}, bf16[2,128,128]{2,1,0:T(8,128)(2,1)S(1)}, u32[]{:S(2)}, u32[]{:S(2)}) collective-permute-start(bf16[2,128,128]{2,1,0:T(8,128)(2,1)S(1)} %get-tuple-element.56), channel_id=1, source_target_pairs={{0,28},{4,24},{8,20},{12,16},{16,12},{20,8},{24,4},{28,0},{1,29},{... | collective-permute-start | bytes 196616 | tf_op jit(solution)/shard_map/ppermute | solution.py:349
  117.9 4.5 %collective-permute-start.19 = (bf16[2,32,128]{2,1,0:T(8,128)(2,1)S(1)}, bf16[2,32,128]{2,1,0:T(8,128)(2,1)S(1)}, u32[]{:S(2)}, u32[]{:S(2)}) collective-permute-start(bf16[2,32,128]{2,1,0:T(8,128)(2,1)S(1)} %get-tuple-element.58), channel_id=1, source_target_pairs={{0,1},{1,0},{2,3},{3,2},{4,5},{5,4},{6,7},{7,6},{8,9},{9,8},{10,11... | collective-permute-start | bytes 49160 | tf_op jit(solution)/shard_map/ppermute | solution.py:349
  119.8 6.6 %collective-permute-start.20 = (bf16[2,32,128]{2,1,0:T(8,128)(2,1)S(1)}, bf16[2,32,128]{2,1,0:T(8,128)(2,1)S(1)}, u32[]{:S(2)}, u32[]{:S(2)}) collective-permute-start(bf16[2,32,128]{2,1,0:T(8,128)(2,1)S(1)} %get-tuple-element.59), channel_id=1, source_target_pairs={{0,2},{1,3},{2,0},{3,1},{4,6},{5,7},{6,4},{7,5},{8,10},{9,11},{10,... | collective-permute-start | bytes 49160 | tf_op jit(solution)/shard_map/ppermute | solution.py:349
  122.2 5.5 %collective-permute-start.21 = (bf16[2,32,128]{2,1,0:T(8,128)(2,1)S(1)}, bf16[2,32,128]{2,1,0:T(8,128)(2,1)S(1)}, u32[]{:S(2)}, u32[]{:S(2)}) collective-permute-start(bf16[2,32,128]{2,1,0:T(8,128)(2,1)S(1)} %get-tuple-element.60), channel_id=1, source_target_pairs={{0,3},{1,2},{2,1},{3,0},{4,7},{5,6},{6,5},{7,4},{8,11},{9,10},{10,... | collective-permute-start | bytes 49160 | tf_op jit(solution)/shard_map/ppermute | solution.py:349
  128.3 4.9 %collective-permute-start.28 = (bf16[4,2,32,128]{3,2,1,0:T(8,128)(2,1)S(1)}, bf16[4,2,32,128]{3,2,1,0:T(8,128)(2,1)S(1)}, u32[]{:S(2)}, u32[]{:S(2)}) collective-permute-start(bf16[4,2,32,128]{3,2,1,0:T(8,128)(2,1)S(1)} %state_order.1.refs_0_), channel_id=1, source_target_pairs={{0,28},{4,24},{8,20},{12,16},{16,12},{20,8},{24,4},{28,0},{1,29},{... | collective-permute-start | bytes 196616 | tf_op jit(solution)/shard_map/ppermute | solution.py:349
  128.4 5.5 %collective-permute-start.27 = (bf16[4,2,32,128]{3,2,1,0:T(8,128)(2,1)S(1)}, bf16[4,2,32,128]{3,2,1,0:T(8,128)(2,1)S(1)}, u32[]{:S(2)}, u32[]{:S(2)}) collective-permute-start(bf16[4,2,32,128]{3,2,1,0:T(8,128)(2,1)S(1)} %state_order.1.refs_0_), channel_id=1, source_target_pairs={{0,24},{4,28},{8,16},{12,20},{16,8},{20,12},{24,0},{28,4},{1,25},{... | collective-permute-start | bytes 196616 | tf_op jit(solution)/shard_map/ppermute | solution.py:349
  130.2 5.6 %collective-permute-start.26 = (bf16[4,2,32,128]{3,2,1,0:T(8,128)(2,1)S(1)}, bf16[4,2,32,128]{3,2,1,0:T(8,128)(2,1)S(1)}, u32[]{:S(2)}, u32[]{:S(2)}) collective-permute-start(bf16[4,2,32,128]{3,2,1,0:T(8,128)(2,1)S(1)} %state_order.1.refs_0_), channel_id=1, source_target_pairs={{0,20},{4,16},{8,28},{12,24},{16,4},{20,0},{24,12},{28,8},{1,21},{... | collective-permute-start | bytes 196616 | tf_op jit(solution)/shard_map/ppermute | solution.py:349
  131.4 5.9 %collective-permute-start.25 = (bf16[4,2,32,128]{3,2,1,0:T(8,128)(2,1)S(1)}, bf16[4,2,32,128]{3,2,1,0:T(8,128)(2,1)S(1)}, u32[]{:S(2)}, u32[]{:S(2)}) collective-permute-start(bf16[4,2,32,128]{3,2,1,0:T(8,128)(2,1)S(1)} %state_order.1.refs_0_), channel_id=1, source_target_pairs={{0,16},{4,20},{8,24},{12,28},{16,0},{20,4},{24,8},{28,12},{1,17},{... | collective-permute-start | bytes 196616 | tf_op jit(solution)/shard_map/ppermute | solution.py:349
  132.8 4.5 %collective-permute-start.24 = (bf16[4,2,32,128]{3,2,1,0:T(8,128)(2,1)S(1)}, bf16[4,2,32,128]{3,2,1,0:T(8,128)(2,1)S(1)}, u32[]{:S(2)}, u32[]{:S(2)}) collective-permute-start(bf16[4,2,32,128]{3,2,1,0:T(8,128)(2,1)S(1)} %state_order.1.refs_0_), channel_id=1, source_target_pairs={{0,12},{4,8},{8,4},{12,0},{16,28},{20,24},{24,20},{28,16},{1,13},{... | collective-permute-start | bytes 196616 | tf_op jit(solution)/shard_map/ppermute | solution.py:349
  133.2 4.8 %collective-permute-start.23 = (bf16[4,2,32,128]{3,2,1,0:T(8,128)(2,1)S(1)}, bf16[4,2,32,128]{3,2,1,0:T(8,128)(2,1)S(1)}, u32[]{:S(2)}, u32[]{:S(2)}) collective-permute-start(bf16[4,2,32,128]{3,2,1,0:T(8,128)(2,1)S(1)} %state_order.1.refs_0_), channel_id=1, source_target_pairs={{0,8},{4,12},{8,0},{12,4},{16,24},{20,28},{24,16},{28,20},{1,9},{5... | collective-permute-start | bytes 196616 | tf_op jit(solution)/shard_map/ppermute | solution.py:349
  133.9 4.1 %collective-permute-start.22 = (bf16[4,2,32,128]{3,2,1,0:T(8,128)(2,1)S(1)}, bf16[4,2,32,128]{3,2,1,0:T(8,128)(2,1)S(1)}, u32[]{:S(2)}, u32[]{:S(2)}) collective-permute-start(bf16[4,2,32,128]{3,2,1,0:T(8,128)(2,1)S(1)} %state_order.1.refs_0_), channel_id=1, source_target_pairs={{0,4},{4,0},{8,12},{12,8},{16,20},{20,16},{24,28},{28,24},{1,5},{5... | collective-permute-start | bytes 196616 | tf_op jit(solution)/shard_map/ppermute | solution.py:349
